TPU v7x, 512 devices: a whole 4x4x16 slice. The times are simulated.
512 devices in a mesh: date: 16 (over x, z_hi), line: 32 (over z_lo, y, core).
Axes of the slice: x: 4, y: 4, z: 16 (z_hi: 4, z_lo: 4; z = z_hi * 4 + z_lo), core: 2. Of those that a mesh axis runs over, the one named last changes fastest.
Arguments:
- reference_slc: float32 [2, 384, 12288], P(None, 'line', 'date'), may hold values from -6 to 6
- secondary_slc: float32 [16, 2, 384, 12288], P('date', None, 'line'), may hold values from -6 to 6
- range_start: int32 [16], P('date'), may hold values from 0 to 12287
- azimuth_start: int32 [16], P('date'), may hold values from 0 to 383
Outputs:
- interferogram: float32 [16, 2, 384, 12288], P('date', None, 'line')
All inputs are finite; a program needn't handle non-finite values.
Results may differ from a plain program's by a relative error of at most 0.0003.
Values sent between devices are 32-bit elements; how exact they have to be, the bound alone decides.
A program may use at most 128 MiB of HBM per device.

v0:
```python
import math

import jax
import jax.numpy as jnp
from jax import lax
from jax.sharding import PartitionSpec as P

RG = 12288
RBAND = 8192


HIGHEST_PRECISION = lax.Precision.HIGHEST


def tables(length, direction):
    counter = jnp.arange(length, dtype=jnp.int32)
    product = counter[:, None] * counter[None, :] % length
    angles = product.astype(jnp.float32) * (direction * 2.0 * math.pi / length)
    return (jnp.cos(angles), jnp.sin(angles))


def block_table(cosine, sine):
    return jnp.stack([jnp.stack([cosine, -sine], 1), jnp.stack([sine, cosine], 1)], 0)


def range_transform(signal, direction):
    length = signal.shape[-1]
    factor_in = 128
    while length % factor_in != 0:
        factor_in = factor_in // 2
    factor_out = length // factor_in
    grid = signal.reshape(signal.shape[:-1] + (factor_out, factor_in))
    outer_block = block_table(*tables(factor_out, direction))
    first = jnp.einsum("akbn,...blnq->...alkq", outer_block, grid, precision=HIGHEST_PRECISION)
    rows_out = jnp.arange(factor_out, dtype=jnp.int32)
    cols_in = jnp.arange(factor_in, dtype=jnp.int32)
    twist = (rows_out[:, None] * cols_in[None, :] % length).astype(jnp.float32) * (
        direction * 2.0 * math.pi / length
    )
    twist_cos = jnp.cos(twist)
    twist_sin = jnp.sin(twist)
    first_real = first[..., 0, :, :, :]
    first_imag = first[..., 1, :, :, :]
    second = jnp.stack(
        [
            first_real * twist_cos - first_imag * twist_sin,
            first_real * twist_sin + first_imag * twist_cos,
        ],
        -4,
    )
    inner_block = block_table(*tables(factor_in, direction))
    third = jnp.einsum("...blkq,ambq->...almk", second, inner_block, precision=HIGHEST_PRECISION)
    return third.reshape(signal.shape)


def doppler_band(signals, azimuth_start, length):
    band_width = length // 2
    fwd_block = block_table(*tables(length, -1.0))
    inv_block = block_table(*tables(length, 1.0))
    doppler_bins = jnp.arange(length, dtype=jnp.int32)
    keep = ((doppler_bins[None, :] - azimuth_start[:, None]) % length < band_width).astype(
        jnp.float32
    ) / length
    spectrum = jnp.einsum("akbn,dsbne->dsake", fwd_block, signals, precision=HIGHEST_PRECISION)
    spectrum = spectrum * keep[:, None, None, :, None]
    output = jnp.einsum("ajbk,dsbke->dsaje", inv_block, spectrum, precision=HIGHEST_PRECISION)
    return output


def body(reference_slc, secondary_slc, range_start, azimuth_start):
    gathered = lax.all_gather(reference_slc, "date", axis=2, tiled=True)
    ref_spec = range_transform(gathered, -1.0)
    sec_spec = range_transform(secondary_slc, -1.0)
    line_rows = secondary_slc.shape[2]
    azimuth_length = line_rows * lax.axis_size("line")
    range_bins = jnp.arange(RG, dtype=jnp.int32)
    range_keep = ((range_bins[None, :] - range_start[:, None]) % RG < RBAND).astype(jnp.float32)
    sec_masked = sec_spec * range_keep[:, None, None, :]
    stacked = jnp.concatenate([ref_spec[None], sec_masked], axis=0)
    columns = lax.all_to_all(stacked, "line", split_axis=3, concat_axis=2, tiled=True)
    width_dev = columns.shape[3]
    column_bins = lax.axis_index("line") * width_dev + jnp.arange(width_dev, dtype=jnp.int32)
    column_keep = ((column_bins[None, :] - range_start[:, None]) % RG < RBAND).astype(jnp.float32)
    ref_columns = columns[0][None] * column_keep[:, None, None, :]
    signals = jnp.stack([ref_columns, columns[1:]], 1)
    filtered = doppler_band(signals, azimuth_start, azimuth_length)
    spectra = lax.all_to_all(filtered, "line", split_axis=3, concat_axis=4, tiled=True)
    back = range_transform(spectra, 1.0)
    scaling = 1.0 / RG
    ref_out_real = back[:, 0, 0] * scaling
    ref_out_imag = back[:, 0, 1] * scaling
    sec_out_real = back[:, 1, 0] * scaling
    sec_out_imag = back[:, 1, 1] * scaling
    cross_real = sec_out_real * ref_out_real + sec_out_imag * ref_out_imag
    cross_imag = sec_out_imag * ref_out_real - sec_out_real * ref_out_imag
    return jnp.stack([cross_real, cross_imag], 1)


def solution(mesh):
    in_specs = (P(None, "line", "date"), P("date", None, "line", None), P("date"), P("date"))
    out_specs = P("date", None, "line", None)
    return jax.shard_map(body, mesh=mesh, in_specs=in_specs, out_specs=out_specs, check_vma=False)
```

profile of v0, /device:TPU:1, one launch (start us, length us, event | category | flops | bytes accessed | tf_op | source)
XLA Modules:
  0.0 443.3 jit_solution(17395026618795754654)
XLA Ops:
  8.5 2.3 reshape.686
  14.5 2.5 reshape.674
  19.5 81.5 %all-gather.2.cloned.1.call-done = f32[2,12,12288]{2,0,1:T(2,128)} async-done(((f32[2,12,768]{2,0,1:T(2,128)}), f32[2,12,12288]{2,0,1:T(2,128)}) %all-gather.2.cloned.1.call-update) | async-done | bytes 1179664 | tf_op jit(solution)/shard_map/all_gather | solution.py:71
  101.0 2.4 reshape.681
  105.6 2.1 convolution_bitcast_fusion.2
  109.5 2.5 broadcast_in_dim_reshape.3
  112.0 2.6 pad_maximum_fusion
  114.6 23.6 %copy.53 = f32[2,2,12,12288]{2,1,0,3:T(2,128)} copy(f32[2,2,12,12288]{3,1,2,0:T(2,128)S(1)} %pad_maximum_fusion) | data formatting | bytes 4718592 | tf_op jit(solution)/shard_map/concatenate | solution.py:79
  138.2 43.3 %reshape.705 = f32[32,1,18432]{2,1,0:T(1,128)} reshape(f32[12288,2,2,12]{3,2,1,0:T(2,128)} %bitcast.223) | data formatting | bytes 4718592
  181.5 8.2 %all-to-all-start = ((f32[32,1,18432]{2,1,0:T(1,128)}), f32[32,1,18432]{2,1,0:T(1,128)S(1)}, u32[]{:S(2)}, u32[]{:S(2)}) async-start(f32[32,1,18432]{2,1,0:T(1,128)} %reshape.705), calls=%async_computation | async-start | bytes 4718592 | tf_op jit(solution)/shard_map/all_to_all | solution.py:80
  190.4 2.3 fusion.46
  192.6 2.3 fusion.45
  194.9 2.4 fusion.38
  197.3 2.4 fusion.40
  202.5 40.8 %all-to-all-done = f32[32,1,18432]{2,1,0:T(1,128)S(1)} async-done(((f32[32,1,18432]{2,1,0:T(1,128)}), f32[32,1,18432]{2,1,0:T(1,128)S(1)}, u32[]{:S(2)}, u32[]{:S(2)}) %all-to-all-start) | async-done | bytes 2359328 | tf_op jit(solution)/shard_map/all_to_all | solution.py:80
  243.8 8.8 %reduce = f32[32,18432]{1,0:T(8,128)} reduce(f32[32,1,18432]{2,1,0:T(1,128)S(1)} %all-to-all-done, f32[]{:T(128)} %broadcast.972), dimensions={1}, to_apply=%all_to_all.22.reduce_sub_computation | reduce | bytes 4718596 | tf_op jit(solution)/shard_map/all_to_all | solution.py:80
  252.7 55.0 %reshape.706 = f32[12288,2,2,12]{3,2,1,0:T(2,128)} reshape(f32[32,18432]{1,0:T(8,128)} %reduce) | data formatting | bytes 4718592
  307.6 20.1 %copy.86 = f32[2,2,12,32,384]{4,3,1,2,0:T(8,128)S(1)} copy(f32[2,2,12,32,384]{2,1,0,4,3:T(2,128)} %bitcast.224) | data formatting | bytes 4718592 | tf_op jit(solution)/shard_map/all_to_all | solution.py:80
  329.8 2.1 copy.56
  332.0 2.2 copy.57
  336.9 6.0 %fusion = f32[2,384,2,384,1]{3,1,4,2,0:T(8,128)S(1)} fusion(f32[1,1,2,384,384]{3,4,2,1,0:T(8,128)S(1)} %copy.58, f32[1,1,2,384,384]{3,4,2,1,0:T(8,128)S(1)} %broadcast_multiply_fusion, f32[1,384,2,384]{3,1,2,0:T(8,128)S(1)} %copy-done, f32[1,384,2,384]{3,1,2,0:T(8,128)S(1)} %get-tuple-element.13), kind=kOutput, calls=%fused_computation.2 | convolution fusion | flops 5436997632 | bytes 7077888 | tf_op jit(solution)/shard_map/akbn,dsbne->dsake/dot_general | solution.py:64
  342.9 5.8 %fusion.18 = f32[1,2,2,384,384]{3,4,2,1,0:T(8,128)S(1)} fusion(f32[1,384,2,384]{3,1,2,0:T(8,128)S(1)} %copy-done.2, f32[1,384,2,384]{3,1,2,0:T(8,128)S(1)} %copy-done.1, f32[2,384,2,384,1]{3,1,4,2,0:T(8,128)S(1)} %fusion, f32[384]{0:T(512)S(1)} %fusion.89), kind=kOutput, calls=%fused_computation.22 | convolution fusion | flops 5436997632 | bytes 7079424 | tf_op jit(solution)/shard_map/ajbk,dsbke->dsaje/dot_general | solution.py:66
  348.8 3.4 copy.59
  352.1 6.4 %all-to-all-start.1 = ((f32[1,2,2,384,384]{4,2,1,0,3:T(2,128)}), f32[1,2,2,384,384]{4,2,1,0,3:T(2,128)S(1)}, u32[]{:S(2)}, u32[]{:S(2)}) async-start(f32[1,2,2,384,384]{4,2,1,0,3:T(2,128)} %copy.59), calls=%async_computation.1 | async-start | bytes 4718592 | tf_op jit(solution)/shard_map/all_to_all | solution.py:87
  359.8 52.5 %all-to-all-done.1 = f32[1,2,2,384,384]{4,2,1,0,3:T(2,128)S(1)} async-done(((f32[1,2,2,384,384]{4,2,1,0,3:T(2,128)}), f32[1,2,2,384,384]{4,2,1,0,3:T(2,128)S(1)}, u32[]{:S(2)}, u32[]{:S(2)}) %all-to-all-start.1) | async-done | bytes 2359328 | tf_op jit(solution)/shard_map/all_to_all | solution.py:87
  415.0 2.3 reshape.696
  417.4 2.3 fusion.14
  420.1 2.0 fusion.17
  422.1 2.3 copy.62
  424.4 4.4 reshape.679
  428.8 2.1 fusion.31
  430.9 2.2 fusion.33
  (69 shorter events, 26.9 us)
Async XLA Ops:
  6.5 94.4 %all-gather.2.cloned.1.call-start = ((), (), s32[]{:S(2)}) async-start(), calls=%async_computation.2 | async-start | bytes 1253376 | tf_op jit(solution)/shard_map/all_gather | solution.py:71
  7.9 4.1 copy-start.11
  7.9 4.1 copy-start.13
  10.8 1.2 copy-start.7
  10.8 1.2 copy-start.9
  12.2 0.7 copy-start.3
  12.2 0.7 copy-start.5
  19.5 84.0 %copy-start.8 = (f32[1,96,2,96]{3,1,2,0:T(8,128)S(1)}, f32[1,96,2,96]{3,1,2,0:T(8,128)}, u32[]{:S(2)}) copy-start(f32[1,96,2,96]{3,1,2,0:T(8,128)} %copy-done.7) | copy-start | bytes 221188
  19.5 84.0 %copy-start.10 = (f32[1,96,2,96]{3,1,2,0:T(8,128)S(1)}, f32[1,96,2,96]{3,1,2,0:T(8,128)}, u32[]{:S(2)}) copy-start(f32[1,96,2,96]{3,1,2,0:T(8,128)} %copy-done.9) | copy-start | bytes 221188
  103.5 1.2 copy-start.12
  103.5 1.2 copy-start.14
  104.7 0.9 copy-start.4
  104.7 1.0 copy-start.6
  181.5 61.7 %all-to-all-start = ((f32[32,1,18432]{2,1,0:T(1,128)}), f32[32,1,18432]{2,1,0:T(1,128)S(1)}, u32[]{:S(2)}, u32[]{:S(2)}) async-start(f32[32,1,18432]{2,1,0:T(1,128)} %reshape.705), calls=%async_computation | async-start | bytes 4718592 | tf_op jit(solution)/shard_map/all_to_all | solution.py:80
  335.3 1.6 copy-start
  336.9 6.0 %copy-start.1 = (f32[1,384,2,384]{3,1,2,0:T(8,128)S(1)}, f32[1,384,2,384]{3,1,2,0:T(8,128)}, u32[]{:S(2)}) copy-start(f32[1,384,2,384]{3,1,2,0:T(8,128)} %get-tuple-element.15) | copy-start | bytes 3538948
  336.9 6.0 %copy-start.2 = (f32[1,384,2,384]{3,1,2,0:T(8,128)S(1)}, f32[1,384,2,384]{3,1,2,0:T(8,128)}, u32[]{:S(2)}) copy-start(f32[1,384,2,384]{3,1,2,0:T(8,128)} %get-tuple-element.16) | copy-start | bytes 3538948
  352.1 60.2 %all-to-all-start.1 = ((f32[1,2,2,384,384]{4,2,1,0,3:T(2,128)}), f32[1,2,2,384,384]{4,2,1,0,3:T(2,128)S(1)}, u32[]{:S(2)}, u32[]{:S(2)}) async-start(f32[1,2,2,384,384]{4,2,1,0,3:T(2,128)} %copy.59), calls=%async_computation.1 | async-start | bytes 4718592 | tf_op jit(solution)/shard_map/all_to_all | solution.py:87
Sparse Core Ops, SparseCore 0:
  10.3 90.6 all-gather.1
where the time goes:
time: 451 us; the launch traced here: 443 us
  local copies, waits for them, and re-layouts  181 us (40%)
  waiting for transfers between devices  175 us (39%)
  other arithmetic  35.4 us (8%)
  matrix products  21.8 us (5%)
  between operations  15.5 us (3%)
  starting transfers between devices  14.6 us (3%)
    unnamed x32, local copies, waits for them, and re-layouts  99.9 us
    all_gather x1, waiting for transfers between devices, body(): gathered = lax.all_gather(reference_slc, 'date', axis=2, tiled=True)  81.5 us
    all_to_all x1, waiting for transfers between devices, body(): lax.all_to_all(filtered, 'line', split_axis=3, concat_axis=4, tiled=True)  52.5 us
    all_to_all x1, waiting for transfers between devices, body(): lax.all_to_all(stacked, 'line', split_axis=3, concat_axis=2, tiled=True)  40.8 us
    concatenate x1, local copies, waits for them, and re-layouts, body(): stacked = jnp.concatenate([ref_spec[None], sec_masked], axis=0)  23.6 us
    all_to_all x2, local copies, waits for them, and re-layouts, body(): lax.all_to_all(stacked, 'line', split_axis=3, concat_axis=2, tiled=True)  20.6 us
  transfers between devices with their start and end apart: 3, of which 3 were waited for; matrix products, arithmetic and copies ran while one was open for 5% of the time, Pallas kernels for 0%

commit v1 on v0

v1 whole, which is shorter than its diff:
```python
import math

import jax
import jax.numpy as jnp
import ml_dtypes
import numpy as np
from jax import lax
from jax.experimental import pallas as pl
from jax.experimental.pallas import tpu as pltpu
from jax.sharding import PartitionSpec as P

RG = 12288
AZ = 384
OUTER = 32
INNER = 384
KEEP = 256
LINES = 12
ROWS = 24
PEERS = 32
MESH = pl.DeviceIdType.MESH
F32 = jnp.float32
BF16 = jnp.bfloat16
VMEM_LIMIT = 56 * 1024 * 1024


def row_line():
    return np.array(list(range(8)) + list(range(8)) + list(range(8, 12)) * 2)


def row_part():
    return np.array([0] * 8 + [1] * 8 + [0] * 4 + [1] * 4)


def dirichlet(offset, width, length):
    offset = np.asarray(offset)
    safe = np.where(offset == 0, 1, offset)
    value = np.sin(np.pi * width * safe / length) / (length * np.sin(np.pi * safe / length))
    return np.where(offset == 0, width / length, value)


def split_table(table):
    table = np.asarray(table, np.float32)
    high = table.astype(ml_dtypes.bfloat16)
    low = (table - high.astype(np.float32)).astype(ml_dtypes.bfloat16)
    return np.stack([high, low])


def azimuth_tables():
    lines = (np.arange(PEERS)[:, None] * LINES + row_line()[None]).reshape(-1)
    part = np.tile(row_part(), PEERS)
    full = dirichlet(lines[:, None] - lines[None, :], AZ // 2, AZ)
    own = full * (part[:, None] == part[None, :])
    return split_table(own), full.astype(np.float32).reshape(4, 192, 768)


def range_tables():
    n2 = np.arange(INNER)
    angle = 2 * np.pi * (np.arange(KEEP // 2)[None, :] + 0.5) * n2[:, None] / INNER
    basis = math.sqrt(2 / INNER) * np.concatenate([np.cos(angle), np.sin(angle)], 1)
    projection = dirichlet(n2[:, None] - n2[None, :], KEEP, INNER)
    return split_table(basis), split_table(basis.T), split_table(projection)


def cmul_const(re, im, angle):
    c, s = math.cos(angle), math.sin(angle)
    if abs(c - 1) < 1e-12:
        return re, im
    if abs(c) < 1e-12:
        return (-im, re) if s > 0 else (im, -re)
    if abs(abs(c) - abs(s)) < 1e-12:
        r = math.sqrt(0.5)
        if c > 0 and s > 0:
            return (re - im) * r, (re + im) * r
        if c > 0:
            return (re + im) * r, (im - re) * r
        if s > 0:
            return (re + im) * -r, (re - im) * r
        return (im - re) * r, (re + im) * -r
    return re * c - im * s, re * s + im * c


def dft_small(values, sign):
    n = len(values)
    if n == 1:
        return values
    even = dft_small(values[0::2], sign)
    odd = dft_small(values[1::2], sign)
    low, high = [], []
    for k in range(n // 2):
        tr, ti = cmul_const(odd[k][0], odd[k][1], sign * 2 * math.pi * k / n)
        low.append((even[k][0] + tr, even[k][1] + ti))
        high.append((even[k][0] - tr, even[k][1] - ti))
    return low + high


def dft32(load, sign):
    middle = []
    for q in range(8):
        part = dft_small([load(q + 8 * p) for p in range(4)], sign)
        middle.append([cmul_const(*part[s], sign * 2 * math.pi * q * s / 32) for s in range(4)])
    out = [None] * 32
    for s in range(4):
        part = dft_small([middle[q][s] for q in range(8)], sign)
        for t in range(8):
            out[s + 4 * t] = part[t]
    return out


def split_value(x):
    high = x.astype(BF16)
    low = (x - high.astype(F32)).astype(BF16)
    return high, low


def dot(a, b):
    return jnp.dot(a, b, preferred_element_type=F32)


def dot3(a, b):
    return dot(a[0], b[0]) + dot(a[1], b[0]) + dot(a[0], b[1])


def forward_kernel(sec_ref, twist_ref, phase_ref, basis_ref, out_ref, mid_ref):
    def chunk(a, _):
        for group in range(2):
            lines = slice(0, 8) if group == 0 else slice(8, 12)
            pc = phase_ref[0, lines, :]
            ps = phase_ref[1, lines, :]

            def load(n1):
                at = pl.ds(pl.multiple_of((n1 * 3 + a) * 128, 128), 128)
                return sec_ref[0, 0, lines, at], sec_ref[0, 1, lines, at]

            for k1, (re, im) in enumerate(dft32(load, -1)):
                c = twist_ref[0, a, k1 : k1 + 1, :]
                s = twist_ref[1, a, k1 : k1 + 1, :]
                re, im = re * c + im * s, im * c - re * s
                re, im = re * pc + im * ps, im * pc - re * ps
                if group == 0:
                    mid_ref[a, k1 * ROWS : k1 * ROWS + 8, :] = re
                    mid_ref[a, k1 * ROWS + 8 : k1 * ROWS + 16, :] = im
                else:
                    mid_ref[a, k1 * ROWS + 16 : k1 * ROWS + 24, :] = jnp.concatenate([re, im], 0)
        return 0

    lax.fori_loop(0, 3, chunk, 0)

    def rows(step, _):
        at = pl.ds(pl.multiple_of(step * 192, 192), 192)
        block = jnp.concatenate([mid_ref[a, at, :] for a in range(3)], 1)
        result = dot3(split_value(block), (basis_ref[0], basis_ref[1]))
        out_ref[pl.ds(step * 8, 8)] = result.reshape(8, ROWS, KEEP)
        return 0

    lax.fori_loop(0, 4, rows, 0)


def forward(sec, twist, phase, basis):
    return pl.pallas_call(
        forward_kernel,
        out_shape=jax.ShapeDtypeStruct((PEERS, ROWS, KEEP), F32),
        scratch_shapes=[pltpu.VMEM((3, PEERS * ROWS, 128), F32)],
        compiler_params=pltpu.CompilerParams(vmem_limit_bytes=VMEM_LIMIT),
        name="range_forward",
    )(sec, twist, phase, basis)


def remote(src, dst, send, recv, date, line):
    return pltpu.make_async_remote_copy(
        src_ref=src, dst_ref=dst, send_sem=send, recv_sem=recv, device_id=(date, line), device_id_type=MESH
    )


def chunk_of(zh, y):
    skip = 3 - y
    return jnp.where(zh > skip, zh - 1, zh), zh != skip


def gather_kernel(
    sec_ref, chunks_ref, vec_ref, spread_ref, all_ref, vecs_ref,
    a_send, a_recv, v_send, v_recv, y_send, y_recv, r_send, r_recv, l_send, l_recv, own_sem,
):
    d, l = lax.axis_index("date"), lax.axis_index("line")
    x, zh = d // 4, d % 4
    zl, u = l // 8, l % 8
    y = u // 2
    z = zh * 4 + zl
    up, down = (z + 1) % 16, (z + 15) % 16
    right = (x * 4 + up // 4, (up % 4) * 8 + u)
    left = (x * 4 + down // 4, (down % 4) * 8 + u)

    barrier = pltpu.get_barrier_semaphore()

    def greet(i, _):
        pl.semaphore_signal(barrier, inc=1, device_id=(d, (l + i) % PEERS), device_id_type=MESH)
        return 0

    lax.fori_loop(1, PEERS, greet, 0)
    for i in range(1, 4):
        pl.semaphore_signal(barrier, inc=1, device_id=((x + i) % 4 * 4 + zh, l), device_id_type=MESH)
    pl.semaphore_signal(barrier, inc=1, device_id=right, device_id_type=MESH)
    pl.semaphore_signal(barrier, inc=1, device_id=left, device_id_type=MESH)
    pl.semaphore_wait(barrier, PEERS - 1 + 3 + 2)

    def y_copy(c, owner, source):
        return remote(
            chunks_ref.at[c],
            all_ref.at[(6 * zh + c) // 8, zl, pl.ds(pl.multiple_of(source * ROWS, 8), ROWS)],
            y_send.at[c], y_recv.at[source], d, zl * 8 + owner,
        )

    mine, valid = chunk_of(zh, y)
    for c in range(6):
        owner = (6 * zh + c) % 8

        @pl.when(owner != u)
        def _():
            y_copy(c, owner, u).start()

        @pl.when(owner == u)
        def _():
            pltpu.make_async_copy(
                chunks_ref.at[c],
                all_ref.at[(6 * zh + c) // 8, zl, pl.ds(pl.multiple_of(u * ROWS, 8), ROWS)],
                own_sem.at[0],
            ).start()

    def v_copy(i):
        return remote(vec_ref, vecs_ref.at[x], v_send.at[i], v_recv.at[x], (x + i) % 4 * 4 + zh, l)

    def v_arrival(i):
        return remote(
            vec_ref, vecs_ref.at[(x + i) % 4], v_send.at[i], v_recv.at[(x + i) % 4], (x + i) % 4 * 4 + zh, l
        )

    for i in range(1, 4):
        v_copy(i).start()
    own_vec = pltpu.make_async_copy(vec_ref, vecs_ref.at[x], own_sem.at[1])
    own_vec.start()
    own_block = pltpu.make_async_copy(sec_ref.at[l], spread_ref.at[l], own_sem.at[2])
    own_block.start()

    def a_copy(i):
        to = (l + i) % PEERS
        return remote(sec_ref.at[to], spread_ref.at[l], a_send.at[i], a_recv.at[l], d, to)

    def a_start(i, _):
        a_copy(i).start()
        return 0

    def y_arrival(i):
        source = (u + i) % 8
        return remote(
            chunks_ref.at[0],
            all_ref.at[mine, zl, pl.ds(pl.multiple_of(source * ROWS, 8), ROWS)],
            y_send.at[0], y_recv.at[source], d, zl * 8 + source,
        )

    lax.fori_loop(1, PEERS, a_start, 0)

    @pl.when(valid)
    def _():
        for i in range(1, 8):
            y_arrival(i).wait_recv()
        pltpu.make_async_copy(
            chunks_ref.at[0],
            all_ref.at[mine, zl, pl.ds(pl.multiple_of(u * ROWS, 8), ROWS)],
            own_sem.at[0],
        ).wait()

    def ring_copy(origin, send, recv, step, to):
        oh, ol = origin // 4, origin % 4
        i, ok = chunk_of(oh, y)
        i = jnp.where(ok, i, 0)
        return ok, remote(all_ref.at[i, ol], all_ref.at[i, ol], send.at[step], recv.at[step], *to)

    def ring(s, _):
        ok, copy = ring_copy((z + 17 - s) % 16, r_send, r_recv, s, right)

        @pl.when(ok)
        def _():
            copy.start()

        ok2, copy2 = ring_copy((z + s - 1) % 16, l_send, l_recv, s, left)

        @pl.when(ok2 & (s < 8))
        def _():
            copy2.start()

        ok3, copy3 = ring_copy((z + 16 - s) % 16, r_send, r_recv, s, left)

        @pl.when(ok3)
        def _():
            copy3.wait_recv()

        ok4, copy4 = ring_copy((z + s) % 16, l_send, l_recv, s, right)

        @pl.when(ok4 & (s < 8))
        def _():
            copy4.wait_recv()

        return 0

    lax.fori_loop(1, 9, ring, 0)

    def ring_sent(s, _):
        ok, copy = ring_copy((z + 17 - s) % 16, r_send, r_recv, s, right)

        @pl.when(ok)
        def _():
            copy.wait_send()

        ok2, copy2 = ring_copy((z + s - 1) % 16, l_send, l_recv, s, left)

        @pl.when(ok2 & (s < 8))
        def _():
            copy2.wait_send()

        return 0

    lax.fori_loop(1, 9, ring_sent, 0)

    for c in range(6):
        owner = (6 * zh + c) % 8

        @pl.when(owner != u)
        def _():
            y_copy(c, owner, u).wait_send()

    for i in range(1, 4):
        v_copy(i).wait_send()
        v_arrival(i).wait_recv()
    own_vec.wait()
    own_block.wait()

    def a_finish(i, _):
        a_copy(i).wait_send()
        source = (l + i) % PEERS
        remote(sec_ref.at[source], spread_ref.at[source], a_send.at[i], a_recv.at[source], d, source).wait_recv()
        return 0

    lax.fori_loop(1, PEERS, a_finish, 0)


def gather(sec_blocks, chunks, vector):
    any_space = pl.BlockSpec(memory_space=pl.ANY)
    dma = pltpu.SemaphoreType.DMA
    return pl.pallas_call(
        gather_kernel,
        out_shape=(
            jax.ShapeDtypeStruct((PEERS, ROWS, KEEP), F32),
            jax.ShapeDtypeStruct((3, 4, 8 * ROWS, 128), F32),
            jax.ShapeDtypeStruct((4, 8, 2 * AZ), F32),
        ),
        in_specs=[any_space] * 3,
        out_specs=(any_space,) * 3,
        scratch_shapes=[
            dma((PEERS,)), dma((PEERS,)), dma((4,)), dma((4,)), dma((6,)), dma((8,)),
            dma((9,)), dma((9,)), dma((9,)), dma((9,)), dma((3,)),
        ],
        compiler_params=pltpu.CompilerParams(collective_id=1, has_side_effects=True),
        name="gather_lines",
    )(sec_blocks, chunks, vector)


def return_kernel(
    sec_ref, ref_ref, spread_ref, lines_ref, a_send, a_recv, x_send, x_recv, own_sem
):
    d, l = lax.axis_index("date"), lax.axis_index("line")
    x, zh = d // 4, d % 4
    zl, u = l // 8, l % 8
    place = x * 8 + u

    def plane(i):
        other = (place + i) % PEERS
        ox, ou = other // 8, other % 8
        return other, ox, ou, ox * 4 + zh, zl * 8 + ou

    barrier = pltpu.get_barrier_semaphore()

    def greet(i, _):
        pl.semaphore_signal(barrier, inc=1, device_id=(d, (l + i) % PEERS), device_id_type=MESH)
        _, _, _, od, ol = plane(i)
        pl.semaphore_signal(barrier, inc=1, device_id=(od, ol), device_id_type=MESH)
        return 0

    lax.fori_loop(1, PEERS, greet, 0)
    pl.semaphore_wait(barrier, 2 * (PEERS - 1))

    own_block = pltpu.make_async_copy(sec_ref.at[l], spread_ref.at[l], own_sem.at[0])
    own_block.start()
    own_lines = pltpu.make_async_copy(ref_ref.at[x, u], lines_ref.at[x, :, u], own_sem.at[1])
    own_lines.start()

    def a_copy(i):
        to = (l + i) % PEERS
        return remote(sec_ref.at[to], spread_ref.at[l], a_send.at[i], a_recv.at[l], d, to)

    def x_copy(i):
        _, ox, ou, od, ol = plane(i)
        return remote(ref_ref.at[ox, ou], lines_ref.at[x, :, u], x_send.at[i], x_recv.at[place], od, ol)

    def start(i, _):
        a_copy(i).start()
        x_copy(i).start()
        return 0

    lax.fori_loop(1, PEERS, start, 0)
    own_block.wait()
    own_lines.wait()

    def finish(i, _):
        a_copy(i).wait_send()
        x_copy(i).wait_send()
        source = (l + i) % PEERS
        remote(sec_ref.at[source], spread_ref.at[source], a_send.at[i], a_recv.at[source], d, source).wait_recv()
        other, ox, ou, od, ol = plane(i)
        remote(ref_ref.at[ox, ou], lines_ref.at[ox, :, ou], x_send.at[i], x_recv.at[other], od, ol).wait_recv()
        return 0

    lax.fori_loop(1, PEERS, finish, 0)


def give_back(sec_blocks, ref_blocks):
    any_space = pl.BlockSpec(memory_space=pl.ANY)
    dma = pltpu.SemaphoreType.DMA
    return pl.pallas_call(
        return_kernel,
        out_shape=(
            jax.ShapeDtypeStruct((PEERS, ROWS, KEEP), F32),
            jax.ShapeDtypeStruct((4, 3, 8, ROWS, 128), F32),
        ),
        in_specs=[any_space] * 2,
        out_specs=(any_space,) * 2,
        scratch_shapes=[dma((PEERS,)), dma((PEERS,)), dma((PEERS,)), dma((PEERS,)), dma((2,))],
        compiler_params=pltpu.CompilerParams(collective_id=2, has_side_effects=True),
        name="return_lines",
    )(sec_blocks, ref_blocks)


def azimuth_kernel(sec_ref, all_ref, vecs_ref, own_ref, full_ref, sec_out, ref_out):
    def sec_rows(step, _):
        at = pl.ds(pl.multiple_of(step * 192, 192), 192)
        result = dot3((own_ref[0, at, :], own_ref[1, at, :]), sec)
        sec_out[pl.ds(step * 8, 8)] = result.reshape(8, ROWS, KEEP)
        return 0

    sec = split_value(sec_ref[...].reshape(PEERS * ROWS, KEEP))
    lax.fori_loop(0, 4, sec_rows, 0)
    samples = split_value(
        jnp.concatenate([all_ref[i].reshape(2 * AZ, 128) for i in range(3)], 1)
    )
    row = lax.broadcasted_iota(jnp.int32, (ROWS, 2 * AZ), 0)
    real = (row < 8) | ((row >= 16) & (row < 20))

    def date(t, _):
        first = vecs_ref[t, 0:1, :]
        second = vecs_ref[t, 1:2, :]
        mixed = jnp.where(real, first, second)
        table = full_ref[...].reshape(8, ROWS, 2 * AZ) * mixed[None]
        result = dot3(split_value(table.reshape(8 * ROWS, 2 * AZ)), samples)
        for i in range(3):
            ref_out[t, :, i] = result[:, i * 128 : (i + 1) * 128].reshape(8, ROWS, 128)
        return 0

    lax.fori_loop(0, 4, date, 0)


def azimuth(spread, every, vectors, own, full):
    return pl.pallas_call(
        azimuth_kernel,
        out_shape=(
            jax.ShapeDtypeStruct((PEERS, ROWS, KEEP), F32),
            jax.ShapeDtypeStruct((4, 8, 3, ROWS, 128), F32),
        ),
        compiler_params=pltpu.CompilerParams(vmem_limit_bytes=VMEM_LIMIT),
        name="azimuth_filter",
    )(spread, every, vectors, own, full)


def final_kernel(sec_ref, lines_ref, twist_ref, inverse_ref, project_ref, out_ref, sec_mid, ref_mid, sec_time):
    def sec_rows(step, _):
        at = pl.ds(pl.multiple_of(step * 192, 192), 192)
        block = split_value(sec_ref[pl.ds(step * 8, 8)].reshape(192, KEEP))
        result = dot3(block, (inverse_ref[0], inverse_ref[1]))
        for a in range(3):
            sec_mid[a, at, :] = result[:, a * 128 : (a + 1) * 128]
        return 0

    lax.fori_loop(0, 4, sec_rows, 0)

    def pair(tile, group):
        return pltpu.roll(tile, 4, 0) if group else None

    def forward_chunk(a, _):
        for group in range(2):

            def load(n1):
                if group == 0:
                    return lines_ref[n1 * 3 + a, 0:8, :], lines_ref[n1 * 3 + a, 8:16, :]
                tile = lines_ref[n1 * 3 + a, 16:24, :]
                return tile, pair(tile, 1)

            for k1, (re, im) in enumerate(dft32(load, -1)):
                c = twist_ref[0, a, k1 : k1 + 1, :]
                s = twist_ref[1, a, k1 : k1 + 1, :]
                re, im = re * c + im * s, im * c - re * s
                base = k1 * ROWS
                if group == 0:
                    ref_mid[a, base : base + 8, :] = re
                    ref_mid[a, base + 8 : base + 16, :] = im
                else:
                    ref_mid[a, base + 16 : base + 24, :] = jnp.concatenate([re[0:4], im[0:4]], 0)
        return 0

    lax.fori_loop(0, 3, forward_chunk, 0)

    def ref_rows(step, _):
        at = pl.ds(pl.multiple_of(step * 192, 192), 192)
        block = jnp.concatenate([ref_mid[a, at, :] for a in range(3)], 1)
        result = dot3(split_value(block), (project_ref[0], project_ref[1]))
        for a in range(3):
            ref_mid[a, at, :] = result[:, a * 128 : (a + 1) * 128]
        return 0

    lax.fori_loop(0, 4, ref_rows, 0)

    def untwist(mid, a, group):
        def load(k1):
            base = k1 * ROWS
            c = twist_ref[0, a, k1 : k1 + 1, :]
            s = twist_ref[1, a, k1 : k1 + 1, :]
            if group == 0:
                re, im = mid[a, base : base + 8, :], mid[a, base + 8 : base + 16, :]
            else:
                re = mid[a, base + 16 : base + 24, :]
                im = pair(re, 1)
            return re * c - im * s, im * c + re * s

        return load

    def last_chunk(a, _):
        for group in range(2):
            count = 8 if group == 0 else 4
            lines = slice(0, 8) if group == 0 else slice(8, 12)
            for n1, (re, im) in enumerate(dft32(untwist(sec_mid, a, group), 1)):
                sec_time[0, n1] = re
                sec_time[1, n1] = im
            for n1, (re, im) in enumerate(dft32(untwist(ref_mid, a, group), 1)):
                sr = sec_time[0, n1] * (1.0 / 1024)
                si = sec_time[1, n1] * (1.0 / 1024)
                at = pl.ds(pl.multiple_of((n1 * 3 + a) * 128, 128), 128)
                out_ref[0, 0, lines, at] = (sr * re + si * im)[0:count]
                out_ref[0, 1, lines, at] = (si * re - sr * im)[0:count]
        return 0

    lax.fori_loop(0, 3, last_chunk, 0)


def final(sec_blocks, lines, twist, inverse, project):
    return pl.pallas_call(
        final_kernel,
        out_shape=jax.ShapeDtypeStruct((1, 2, LINES, RG), F32),
        scratch_shapes=[
            pltpu.VMEM((3, PEERS * ROWS, 128), F32),
            pltpu.VMEM((3, PEERS * ROWS, 128), F32),
            pltpu.VMEM((2, OUTER, 8, 128), F32),
        ],
        compiler_params=pltpu.CompilerParams(vmem_limit_bytes=VMEM_LIMIT),
        name="range_final",
    )(sec_blocks, lines, twist, inverse, project)


def body(reference_slc, secondary_slc, range_start, azimuth_start):
    own, full = azimuth_tables()
    basis, inverse, project = range_tables()
    line = lax.axis_index("line")

    first = range_start[0] + (jnp.arange(OUTER, dtype=jnp.int32) - range_start[0]) % OUTER
    turns = (first + OUTER * (KEEP - 1) // 2)[None, :, None] * jnp.arange(INNER, dtype=jnp.int32).reshape(3, 1, 128)
    angle = (turns % RG).astype(F32) * (2 * math.pi / RG)
    twist = jnp.stack([jnp.cos(angle), jnp.sin(angle)])

    step = 2 * azimuth_start[0] + AZ // 2 - 1

    def phases(lines):
        angle = ((step * lines) % (2 * AZ)).astype(F32) * (math.pi / AZ)
        return jnp.cos(angle), jnp.sin(angle)

    own_cos, own_sin = phases(line * LINES + jnp.arange(LINES, dtype=jnp.int32))
    phase = jnp.broadcast_to(jnp.stack([own_cos, own_sin])[:, :, None], (2, LINES, 128))
    all_rows = (np.arange(PEERS)[:, None] * LINES + row_line()[None]).reshape(-1).astype(np.int32)
    all_real = np.tile(row_part() == 0, PEERS)
    row_cos, row_sin = phases(jnp.asarray(all_rows))
    vector = jnp.stack([jnp.where(all_real, row_cos, row_sin), jnp.where(all_real, -row_sin, row_cos)])
    vector = jnp.pad(vector, ((0, 6), (0, 0)))

    parts = reference_slc.reshape(2, LINES, 6, 128).transpose(2, 0, 1, 3)
    chunks = jnp.concatenate([parts[:, 0, :8], parts[:, 1, :8], parts[:, 0, 8:], parts[:, 1, 8:]], 1)

    full_here = lax.dynamic_index_in_dim(jnp.asarray(full), line // 8, 0, keepdims=False)
    coefficients = forward(secondary_slc, twist, phase, jnp.asarray(basis))
    spread, every, vectors = gather(coefficients, chunks, vector)
    filtered, ref_filtered = azimuth(spread, every, vectors, jnp.asarray(own), full_here)
    returned, lines = give_back(filtered, ref_filtered)
    lines = lines.reshape(96, ROWS, 128)
    return final(returned, lines, twist, jnp.asarray(inverse), jnp.asarray(project))


def solution(mesh):
    in_specs = (P(None, "line", "date"), P("date", None, "line", None), P("date"), P("date"))
    out_specs = P("date", None, "line", None)
    return jax.shard_map(body, mesh=mesh, in_specs=in_specs, out_specs=out_specs, check_vma=False)
```

time: 451 us -> 137 us (0.30); the launches traced: 443 us -> 136 us
  waiting for transfers between devices: 175 us -> 0 us
  local copies, waits for them, and re-layouts: 181 us -> 8.77 us
  Pallas kernels: 0 us -> 123 us
  other arithmetic: 35.4 us -> 3.04 us
  matrix products: 21.8 us -> 0 us
  starting transfers between devices: 14.6 us -> 0 us
  between operations: 15.5 us -> 1.48 us
    pallas_call x0 -> x5, Pallas kernels: none -> 123 us  [the longest x1 61.3 us: gather(): pl.pallas_call(gather_kernel, out_shape=(jax.ShapeDtypeStruct((PEERS, ROW...]
    unnamed x32 -> x3, local copies, waits for them, and re-layouts: 99.9 us -> 1.86 us
    all_to_all x2 -> x0, waiting for transfers between devices: 93.3 us -> none  [the longest x1 52.5 us: body(): lax.all_to_all(filtered, 'line', split_axis=3, concat_axis=4, tiled=True)]
    all_gather x1 -> x0, waiting for transfers between devices: 81.5 us -> none  [body(): gathered = lax.all_gather(reference_slc, 'date', axis=2, tiled=True)]
    concatenate x1 -> x0, local copies, waits for them, and re-layouts: 23.6 us -> none  [body(): stacked = jnp.concatenate([ref_spec[None], sec_masked], axis=0)]
    all_to_all x4 -> x0, local copies, waits for them, and re-layouts: 23.3 us -> none  [the longest x2 20.6 us: body(): lax.all_to_all(stacked, 'line', split_axis=3, concat_axis=2, tiled=True)]
    dot_general x8 -> x0, matrix products: 21.8 us -> none  [the longest x1 5.98 us: doppler_band(): jnp.einsum('akbn,dsbne->dsake', fwd_block, signals, precision=HIGHEST_PRE...]
    all_to_all x2 -> x0, starting transfers between devices: 14.6 us -> none  [the longest x1 8.19 us: body(): lax.all_to_all(stacked, 'line', split_axis=3, concat_axis=2, tiled=True)]
  transfers between devices with their start and end apart: 3 -> 0, of which waited for: 3 -> 0; matrix products, arithmetic and copies ran while one was open for 5% -> 0% of each run, Pallas kernels for 0% -> 0%
where the time goes in v1:
time: 137 us; the launch traced here: 136 us
  Pallas kernels  123 us (90%)
  local copies, waits for them, and re-layouts  8.77 us (6%)
  other arithmetic  3.04 us (2%)
  between operations  1.48 us (1%)
    pallas_call x1, Pallas kernels, gather(): pl.pallas_call(gather_kernel, out_shape=(jax.ShapeDtypeStruct((PEERS, ROW...  61.3 us
    pallas_call x1, Pallas kernels, give_back(): pl.pallas_call(return_kernel, out_shape=(jax.ShapeDtypeStruct((PEERS, ROW...  41.5 us
    pallas_call x1, Pallas kernels, final(): pl.pallas_call(final_kernel, out_shape=jax.ShapeDtypeStruct((1, 2, LINES,...  7.98 us
    pallas_call x1, Pallas kernels, azimuth(): pl.pallas_call(azimuth_kernel, out_shape=(jax.ShapeDtypeStruct((PEERS, RO...  7.86 us
    pallas_call x1, Pallas kernels, forward(): pl.pallas_call(forward_kernel, out_shape=jax.ShapeDtypeStruct((PEERS, ROW...  4.48 us
    pallas_call x1, local copies, waits for them, and re-layouts, final(): pl.pallas_call(final_kernel, out_shape=jax.ShapeDtypeStruct((1, 2, LINES,...  3.33 us

profile of v1, /device:TPU:1, one launch (start us, length us, event | category | flops | bytes accessed | tf_op | source)
XLA Modules:
  0.0 136.4 jit_solution(11263066298195640412)
XLA Ops:
  0.0 0.0 copy-start
  1.4 0.1 fusion.20
  1.5 0.8 fusion.13
  2.3 0.7 broadcast_in_dim.2.phase_ref
  3.0 0.6 select_maximum_fusion.vec_ref
  3.6 0.3 fusion.5
  3.9 0.6 pad_maximum_fusion.twist_ref
  4.5 0.9 reshape.125
  5.5 0.6 pad_maximum_fusion.1.chunks_ref
  6.2 1.9 %dynamic-slice_bitcast_fusion.full_ref = f32[192,768]{1,0:T(8,128)} fusion(f32[4,192,768]{2,1,0:T(8,128)} %constant.108.clone, s32[]{:T(128)S(6)} %select_n.73), kind=kLoop, calls=%fused_computation | loop fusion | bytes 1179652 | tf_op jit(solution)/shard_map/jit(dynamic_index_in_dim)/squeeze | solution.py:601
  8.1 0.0 copy-done
  8.1 1.9 %copy.14.sec_ref = f32[1,2,12,12288]{3,2,1,0:T(8,128)} copy(f32[1,2,12,12288]{3,1,2,0:T(2,128)S(1)} %copy-done) | data formatting | bytes 2359296 | tf_op args[1]
  9.9 4.5 %range_forward.1.sec_ref = f32[32,24,256]{2,1,0:T(8,128)} custom-call(f32[1,2,12,12288]{3,2,1,0:T(8,128)} %copy.14.sec_ref, f32[2,3,32,128]{3,2,1,0:T(8,128)} %pad_maximum_fusion.twist_ref, f32[2,12,128]{2,1,0:T(8,128)} %broadcast_in_dim.2.phase_ref, bf16[2,384,256]{2,1,0:T(8,128)(2,1)} %constant.109.clone.basis_ref), custom_call_target="tpu_custom_call" | custom-call | tf_op jit(solution)/shard_map/range_forward/pallas_call | solution.py:159
  14.4 61.3 %gather_lines.1 = (f32[32,24,256]{2,1,0:T(8,128)}, f32[3,4,192,128]{3,2,1,0:T(8,128)}, f32[4,8,768]{2,1,0:T(8,128)}) custom-call(f32[32,24,256]{2,1,0:T(8,128)} %range_forward.1.sec_ref, f32[6,24,128]{2,1,0:T(8,128)} %pad_maximum_fusion.1.chunks_ref, f32[8,768]{1,0:T(8,128)} %select_maximum_fusion.vec_ref), custom_call_target="tpu_custom_call" | custom-call | tf_op jit(solution)/shard_map/gather_lines/pallas_call | solution.py:348
  75.7 7.9 %azimuth_filter.1 = (f32[32,24,256]{2,1,0:T(8,128)}, f32[4,8,3,24,128]{4,3,2,1,0:T(8,128)}) custom-call(f32[32,24,256]{2,1,0:T(8,128)} %get-tuple-element.12.sec_ref, f32[3,4,192,128]{3,2,1,0:T(8,128)} %get-tuple-element.13.all_ref, f32[4,8,768]{2,1,0:T(8,128)} %get-tuple-element.14.vecs_ref, bf16[2,768,768]{2,1,0:T(8,128)(2,1)} %constant.110.clone.own_ref, ...), custom_call_target="tpu_custom_call" | custom-call | tf_op jit(solution)/shard_map/azimuth_filter/pallas_call | solution.py:470
  83.6 41.5 %return_lines.1 = (f32[32,24,256]{2,1,0:T(8,128)}, f32[4,3,8,24,128]{4,3,2,1,0:T(8,128)}) custom-call(f32[32,24,256]{2,1,0:T(8,128)} %get-tuple-element.15.sec_ref, f32[4,8,3,24,128]{4,3,2,1,0:T(8,128)} %get-tuple-element.16.ref_ref), custom_call_target="tpu_custom_call" | custom-call | tf_op jit(solution)/shard_map/return_lines/pallas_call | solution.py:427
  125.1 8.0 %range_final.1 = f32[1,2,12,12288]{3,2,1,0:T(8,128)} custom-call(f32[32,24,256]{2,1,0:T(8,128)} %get-tuple-element.17.sec_ref, f32[96,24,128]{2,1,0:T(8,128)} %bitcast.19, f32[2,3,32,128]{3,2,1,0:T(8,128)} %pad_maximum_fusion.twist_ref, bf16[2,256,384]{2,1,0:T(8,128)(2,1)} %constant.111.clone.inverse_ref, bf16[2,384,384]{2,1,0:T(8,128)(2,1)} %constant.112.clone.project_ref), custom_call_target="tpu_custom_call" | custom-call | tf_op jit(solution)/shard_map/range_final/pallas_call | solution.py:561
  133.0 3.3 %copy.16 = f32[1,2,12,12288]{3,1,2,0:T(2,128)} copy(f32[1,2,12,12288]{3,2,1,0:T(8,128)} %range_final.1) | data formatting | bytes 2359296 | tf_op jit(solution)/shard_map/range_final/pallas_call | solution.py:561
  (8 shorter events, 0.1 us)
Async XLA Ops:
  0.0 8.1 %copy-start = (f32[1,2,12,12288]{3,1,2,0:T(2,128)S(1)}, f32[1,2,12,12288]{3,1,2,0:T(2,128)}, u32[]{:S(2)}) copy-start(f32[1,2,12,12288]{3,1,2,0:T(2,128)} %param.12) | copy-start | bytes 3538948

commit v2 on v0

v2 whole, which is shorter than its diff:
```python
import math

import jax
import jax.numpy as jnp
import ml_dtypes
import numpy as np
from jax import lax
from jax.experimental import pallas as pl
from jax.experimental.pallas import tpu as pltpu
from jax.sharding import PartitionSpec as P

RG = 12288
AZ = 384
OUTER = 32
INNER = 384
KEEP = 256
LINES = 12
ROWS = 24
PEERS = 32
MESH = pl.DeviceIdType.MESH
F32 = jnp.float32
BF16 = jnp.bfloat16
VMEM_LIMIT = 56 * 1024 * 1024


def row_line():
    return np.array(list(range(8)) + list(range(8)) + list(range(8, 12)) * 2)


def row_part():
    return np.array([0] * 8 + [1] * 8 + [0] * 4 + [1] * 4)


def dirichlet(offset, width, length):
    offset = np.asarray(offset)
    safe = np.where(offset == 0, 1, offset)
    value = np.sin(np.pi * width * safe / length) / (length * np.sin(np.pi * safe / length))
    return np.where(offset == 0, width / length, value)


def split_table(table):
    table = np.asarray(table, np.float32)
    high = table.astype(ml_dtypes.bfloat16)
    low = (table - high.astype(np.float32)).astype(ml_dtypes.bfloat16)
    return np.stack([high, low])


def azimuth_tables():
    lines = (np.arange(PEERS)[:, None] * LINES + row_line()[None]).reshape(-1)
    part = np.tile(row_part(), PEERS)
    full = dirichlet(lines[:, None] - lines[None, :], AZ // 2, AZ)
    own = full * (part[:, None] == part[None, :])
    return split_table(own), full.astype(np.float32).reshape(4, 192, 768)


def range_tables():
    n2 = np.arange(INNER)
    angle = 2 * np.pi * (np.arange(KEEP // 2)[None, :] + 0.5) * n2[:, None] / INNER
    basis = math.sqrt(2 / INNER) * np.concatenate([np.cos(angle), np.sin(angle)], 1)
    projection = dirichlet(n2[:, None] - n2[None, :], KEEP, INNER)
    return split_table(basis), split_table(basis.T), split_table(projection)


def cmul_const(re, im, angle):
    c, s = math.cos(angle), math.sin(angle)
    if abs(c - 1) < 1e-12:
        return re, im
    if abs(c) < 1e-12:
        return (-im, re) if s > 0 else (im, -re)
    if abs(abs(c) - abs(s)) < 1e-12:
        r = math.sqrt(0.5)
        if c > 0 and s > 0:
            return (re - im) * r, (re + im) * r
        if c > 0:
            return (re + im) * r, (im - re) * r
        if s > 0:
            return (re + im) * -r, (re - im) * r
        return (im - re) * r, (re + im) * -r
    return re * c - im * s, re * s + im * c


def dft_small(values, sign):
    n = len(values)
    if n == 1:
        return values
    even = dft_small(values[0::2], sign)
    odd = dft_small(values[1::2], sign)
    low, high = [], []
    for k in range(n // 2):
        tr, ti = cmul_const(odd[k][0], odd[k][1], sign * 2 * math.pi * k / n)
        low.append((even[k][0] + tr, even[k][1] + ti))
        high.append((even[k][0] - tr, even[k][1] - ti))
    return low + high


def dft32(load, sign):
    middle = []
    for q in range(8):
        part = dft_small([load(q + 8 * p) for p in range(4)], sign)
        middle.append([cmul_const(*part[s], sign * 2 * math.pi * q * s / 32) for s in range(4)])
    out = [None] * 32
    for s in range(4):
        part = dft_small([middle[q][s] for q in range(8)], sign)
        for t in range(8):
            out[s + 4 * t] = part[t]
    return out


def split_value(x):
    high = x.astype(BF16)
    low = (x - high.astype(F32)).astype(BF16)
    return high, low


def dot(a, b):
    return jnp.dot(a, b, preferred_element_type=F32)


def dot3(a, b):
    return dot(a[0], b[0]) + dot(a[1], b[0]) + dot(a[0], b[1])


TWIST, VECTOR, PHASE, TRIG = 0, 192, 208, 240


def trig_tables():
    index = np.zeros((TRIG, 128), np.int32)
    residue = np.full((TRIG, 128), -1, np.int32)
    offset = np.zeros((TRIG, 128), np.int32)
    for part in range(2):
        for a in range(3):
            for k1 in range(OUTER):
                row = part * 96 + a * OUTER + k1
                index[row] = a * 128 + np.arange(128)
                residue[row] = k1
                offset[row] = -part * RG // 4
    lines = (np.arange(PEERS)[:, None] * LINES + row_line()[None]).reshape(6, 128)
    real = np.tile(row_part() == 0, PEERS).reshape(6, 128)
    index[VECTOR : VECTOR + 6] = lines
    offset[VECTOR : VECTOR + 6] = np.where(real, 0, -RG // 4)
    index[VECTOR + 8 : VECTOR + 14] = lines
    offset[VECTOR + 8 : VECTOR + 14] = np.where(real, RG // 4, 0)
    for part in range(2):
        for i in range(LINES):
            row = PHASE + part * 16 + i
            index[row] = i
            residue[row] = -2
            offset[row] = -part * RG // 4
    return index, residue, offset


def trig_values(range_first, azimuth_first, line):
    index, residue, offset = (jnp.asarray(t) for t in trig_tables())
    index = jnp.where(residue == -2, index + line * LINES, index)
    bins = range_first + (residue - range_first) % OUTER + OUTER * (KEEP - 1) // 2
    factor = jnp.where(residue >= 0, bins, (RG // (2 * AZ)) * (2 * azimuth_first + AZ // 2 - 1))
    turns = (factor * index + offset) % RG
    return jnp.cos(turns.astype(F32) * (2 * math.pi / RG))


def remote(src, dst, send, recv, date, line):
    return pltpu.make_async_remote_copy(
        src_ref=src, dst_ref=dst, send_sem=send, recv_sem=recv, device_id=(date, line), device_id_type=MESH
    )


def chunk_of(zh, y):
    skip = 3 - y
    return jnp.where(zh > skip, zh - 1, zh), zh != skip


def twiddle(trig_ref, a, k1):
    row = a * OUTER + k1
    return trig_ref[pl.ds(row, 1), :], trig_ref[pl.ds(96 + row, 1), :]


PIECES = 2
PIECE = 8 * ROWS // PIECES
STEPS = 8


def exchange_kernel(
    sec_ref, refr_ref, trig_ref, basis_ref, own_hbm, full_hbm, back_ref, lines_ref,
    mid_ref, coef_ref, spread_ref, chunks_ref, all_ref, vecs_ref, filt_ref, rout_ref, own_ref, full_ref,
    a_send, a_recv, b_send, b_recv, x_send, x_recv, v_send, v_recv, y_send, y_recv,
    r_send, r_recv, l_send, l_recv, own_sem,
):
    d, l = lax.axis_index("date"), lax.axis_index("line")
    x, zh = d // 4, d % 4
    zl, u = l // 8, l % 8
    y = u // 2
    z = zh * 4 + zl
    up, down = (z + 1) % 16, (z + 15) % 16
    right = (x * 4 + up // 4, (up % 4) * 8 + u)
    left = (x * 4 + down // 4, (down % 4) * 8 + u)
    place = x * 8 + u
    mine, valid = chunk_of(zh, y)

    own_copy = pltpu.make_async_copy(own_hbm, own_ref, own_sem.at[4])
    own_copy.start()
    full_copy = pltpu.make_async_copy(full_hbm.at[zl], full_ref, own_sem.at[5])
    full_copy.start()

    def plane(i):
        other = (place + i) % PEERS
        ox, ou = other // 8, other % 8
        return other, ox, ou, ox * 4 + zh, zl * 8 + ou

    barrier = pltpu.get_barrier_semaphore()

    def greet(i, _):
        pl.semaphore_signal(barrier, inc=1, device_id=(d, (l + i) % PEERS), device_id_type=MESH)
        _, _, _, od, ol = plane(i)
        pl.semaphore_signal(barrier, inc=1, device_id=(od, ol), device_id_type=MESH)
        return 0

    pl.semaphore_signal(barrier, inc=1, device_id=right, device_id_type=MESH)
    pl.semaphore_signal(barrier, inc=1, device_id=left, device_id_type=MESH)
    lax.fori_loop(1, PEERS, greet, 0)

    for c in range(6):
        for part in range(2):
            chunks_ref[c, part * 8 : part * 8 + 8, :] = refr_ref[pl.ds(c * 2 + part, 8, stride=12), :]
            chunks_ref[c, 16 + part * 4 : 20 + part * 4, :] = refr_ref[pl.ds(96 + c * 2 + part, 4, stride=12), :]

    pl.semaphore_wait(barrier, 2 * (PEERS - 1) + 2)

    def y_slot(i, source):
        return all_ref.at[i, zl, pl.ds(pl.multiple_of(source * ROWS, 8), ROWS)]

    def y_copy(c):
        q = 6 * zh + c
        return remote(chunks_ref.at[c], y_slot(q // 8, u), y_send.at[c], y_recv.at[u], d, zl * 8 + q % 8)

    def y_own(c):
        return pltpu.make_async_copy(chunks_ref.at[c], y_slot((6 * zh + c) // 8, u), own_sem.at[0])

    for c in range(6):
        owner = (6 * zh + c) % 8

        @pl.when(owner != u)
        def _():
            y_copy(c).start()

        @pl.when(owner == u)
        def _():
            y_own(c).start()

    def v_copy(i, slot):
        return remote(
            trig_ref.at[pl.ds(VECTOR, 16)], vecs_ref.at[slot], v_send.at[i], v_recv.at[slot],
            (x + i) % 4 * 4 + zh, l,
        )

    for i in range(1, 4):
        v_copy(i, x).start()
    own_vec = pltpu.make_async_copy(trig_ref.at[pl.ds(VECTOR, 16)], vecs_ref.at[x], own_sem.at[1])
    own_vec.start()

    def chunk(a, _):
        for group in range(2):
            rows = 8 if group == 0 else 4
            first = 8 * group
            pc = trig_ref[PHASE + first : PHASE + first + rows, :]
            ps = trig_ref[PHASE + 16 + first : PHASE + 16 + first + rows, :]

            def load(n1):
                at = first * 192 + (n1 * 3 + a) * 2
                return sec_ref[pl.ds(at, rows, stride=192), :], sec_ref[pl.ds(at + 1, rows, stride=192), :]

            for k1, (re, im) in enumerate(dft32(load, -1)):
                c, s = twiddle(trig_ref, a, k1)
                re, im = re * c + im * s, im * c - re * s
                re, im = re * pc + im * ps, im * pc - re * ps
                if group == 0:
                    mid_ref[a, k1 * ROWS : k1 * ROWS + 8, :] = re
                    mid_ref[a, k1 * ROWS + 8 : k1 * ROWS + 16, :] = im
                else:
                    mid_ref[a, k1 * ROWS + 16 : k1 * ROWS + 24, :] = jnp.concatenate([re, im], 0)
        return 0

    def ring_copy(origin, send, recv, step, piece, to):
        i, ok = chunk_of(origin // 4, y)
        ref = all_ref.at[jnp.where(ok, i, 0), origin % 4, pl.ds(pl.multiple_of(piece * PIECE, 8), PIECE)]
        at = step * PIECES + piece
        return ok, remote(ref, ref, send.at[at], recv.at[at], *to)

    def ring_start(s, p):
        ok, copy = ring_copy((z + 17 - s) % 16, r_send, r_recv, s, p, right)
        pl.when(ok)(copy.start)
        ok2, copy2 = ring_copy((z + s - 1) % 16, l_send, l_recv, s, p, left)
        pl.when(ok2 & (s < STEPS))(copy2.start)

    def ring_sent(j, _):
        s, p = 1 + j // PIECES, j % PIECES
        ok, copy = ring_copy((z + 17 - s) % 16, r_send, r_recv, s, p, right)
        pl.when(ok)(copy.wait_send)
        ok2, copy2 = ring_copy((z + s - 1) % 16, l_send, l_recv, s, p, left)
        pl.when(ok2 & (s < STEPS))(copy2.wait_send)
        return 0

    def ring_arrived(s, p):
        ok, copy = ring_copy((z + 16 - s) % 16, r_send, r_recv, s, p, left)
        pl.when(ok)(copy.wait_recv)
        ok2, copy2 = ring_copy((z + s) % 16, l_send, l_recv, s, p, right)
        pl.when(ok2 & (s < STEPS))(copy2.wait_recv)

    def a_copy(i):
        to = (l + i) % PEERS
        return remote(coef_ref.at[to], spread_ref.at[l], a_send.at[i], a_recv.at[l], d, to)

    chunk(0, 0)

    @pl.when(valid)
    def _():
        for i in range(1, 8):
            source = (u + i) % 8
            remote(
                chunks_ref.at[0], y_slot(mine, source), y_send.at[0], y_recv.at[source], d, zl * 8 + source
            ).wait_recv()
        y_own(0).wait()

    for p in range(PIECES):
        ring_start(1, p)

    lax.fori_loop(1, 3, chunk, 0)

    for p in range(PIECES):
        ring_arrived(1, p)
        ring_start(2, p)

    def rows(step, _):
        at = pl.ds(pl.multiple_of(step * 192, 192), 192)
        block = jnp.concatenate([mid_ref[a, at, :] for a in range(3)], 1)
        result = dot3(split_value(block), (basis_ref[0], basis_ref[1]))
        coef_ref[pl.ds(step * 8, 8)] = result.reshape(8, ROWS, KEEP)
        return 0

    lax.fori_loop(0, 4, rows, 0)
    own_block = pltpu.make_async_copy(coef_ref.at[l], spread_ref.at[l], own_sem.at[2])
    own_block.start()

    def a_start(i, _):
        a_copy(i).start()
        return 0

    def ring(j, _):
        s, p = 2 + j // PIECES, j % PIECES
        ring_arrived(s, p)
        ring_start(s + 1, p)
        lax.fori_loop(1 + j * 31 // (6 * PIECES), 1 + (j + 1) * 31 // (6 * PIECES), a_start, 0)
        return 0

    lax.fori_loop(0, 6 * PIECES, ring, 0)
    for p in range(PIECES):
        ring_arrived(STEPS, p)
    lax.fori_loop(0, STEPS * PIECES, ring_sent, 0)
    for i in range(1, 4):
        v_copy(i, x).wait_send()
        v_copy(i, (x + i) % 4).wait_recv()
    own_vec.wait()
    full_copy.wait()

    samples = split_value(jnp.concatenate([all_ref[i].reshape(2 * AZ, 128) for i in range(3)], 1))
    row = lax.broadcasted_iota(jnp.int32, (ROWS, 128), 0)
    real = (row < 8) | ((row >= 16) & (row < 20))

    def x_copy(t, ou):
        return remote(
            rout_ref.at[t, ou], lines_ref.at[x, :, u], x_send.at[t * 8 + ou], x_recv.at[place],
            t * 4 + zh, zl * 8 + ou,
        )

    def x_own():
        return pltpu.make_async_copy(rout_ref.at[x, u], lines_ref.at[x, :, u], own_sem.at[3])

    def date(k, _):
        t = (x + 1 + k) % 4
        parts = []
        for j in range(6):
            mixed = jnp.where(real, vecs_ref[t, j : j + 1, :], vecs_ref[t, 8 + j : 9 + j, :])
            part = full_ref[:, j * 128 : (j + 1) * 128].reshape(8, ROWS, 128) * mixed[None]
            parts.append(part.reshape(8 * ROWS, 128))
        result = dot3(split_value(jnp.concatenate(parts, 1)), samples)
        for i in range(3):
            rout_ref[t, :, i] = result[:, i * 128 : (i + 1) * 128].reshape(8, ROWS, 128)

        def send(i, _):
            ou = (u + i) % 8
            away = (t != x) | (ou != u)
            pl.when(away)(x_copy(t, ou).start)
            return 0

        lax.fori_loop(0, 8, send, 0)
        return 0

    lax.fori_loop(0, 4, date, 0)
    x_own().start()

    def a_finish(i, _):
        a_copy(i).wait_send()
        source = (l + i) % PEERS
        remote(coef_ref.at[source], spread_ref.at[source], a_send.at[i], a_recv.at[source], d, source).wait_recv()
        return 0

    own_block.wait()
    own_copy.wait()
    lax.fori_loop(1, PEERS, a_finish, 0)
    sec = split_value(spread_ref[...].reshape(PEERS * ROWS, KEEP))

    def b_copy(to):
        return remote(filt_ref.at[to], back_ref.at[l], b_send.at[to], b_recv.at[l], d, to)

    def b_own():
        return pltpu.make_async_copy(filt_ref.at[l], back_ref.at[l], own_sem.at[2])

    def sec_rows(k, _):
        step = (zl + 1 + k) % 4
        at = pl.ds(pl.multiple_of(step * 192, 192), 192)
        result = dot3((own_ref[0, at, :], own_ref[1, at, :]), sec)
        filt_ref[pl.ds(step * 8, 8)] = result.reshape(8, ROWS, KEEP)

        def send(i, _):
            to = step * 8 + (u + i) % 8
            pl.when(to != l)(b_copy(to).start)
            return 0

        lax.fori_loop(0, 8, send, 0)
        return 0

    lax.fori_loop(0, 4, sec_rows, 0)
    b_own().start()

    for c in range(6):
        owner = (6 * zh + c) % 8

        @pl.when(owner != u)
        def _():
            y_copy(c).wait_send()

    def finish(i, _):
        other, ox, ou, od, ol = plane(i)
        x_copy(ox, ou).wait_send()
        remote(rout_ref.at[ox, ou], lines_ref.at[ox, :, ou], x_send.at[other], x_recv.at[other], od, ol).wait_recv()
        source = (l + i) % PEERS
        b_copy(source).wait_send()
        remote(filt_ref.at[source], back_ref.at[source], b_send.at[source], b_recv.at[source], d, source).wait_recv()
        return 0

    x_own().wait()
    b_own().wait()
    lax.fori_loop(1, PEERS, finish, 0)


def exchange(sec, ref, trig, basis, own, full):
    any_space = pl.BlockSpec(memory_space=pl.ANY)
    vmem = pl.BlockSpec(memory_space=pltpu.VMEM)
    dma = pltpu.SemaphoreType.DMA
    blocks = (PEERS, ROWS, KEEP)
    ring = (STEPS + 1) * PIECES
    return pl.pallas_call(
        exchange_kernel,
        out_shape=(jax.ShapeDtypeStruct(blocks, F32), jax.ShapeDtypeStruct((4, 3, 8, ROWS, 128), F32)),
        in_specs=[vmem] * 4 + [any_space] * 2,
        out_specs=(any_space,) * 2,
        scratch_shapes=[
            pltpu.VMEM((3, PEERS * ROWS, 128), F32),
            pltpu.VMEM(blocks, F32),
            pltpu.VMEM(blocks, F32),
            pltpu.VMEM((6, ROWS, 128), F32),
            pltpu.VMEM((3, 4, 8 * ROWS, 128), F32),
            pltpu.VMEM((4, 16, 128), F32),
            pltpu.VMEM(blocks, F32),
            pltpu.VMEM((4, 8, 3, ROWS, 128), F32),
            pltpu.VMEM((2, 2 * AZ, 2 * AZ), BF16),
            pltpu.VMEM((8 * ROWS, 2 * AZ), F32),
            dma((PEERS,)), dma((PEERS,)), dma((PEERS,)), dma((PEERS,)), dma((PEERS,)), dma((PEERS,)),
            dma((4,)), dma((4,)), dma((6,)), dma((8,)),
            dma((ring,)), dma((ring,)), dma((ring,)), dma((ring,)), dma((6,)),
        ],
        compiler_params=pltpu.CompilerParams(
            collective_id=1, has_side_effects=True, vmem_limit_bytes=VMEM_LIMIT
        ),
        name="exchange",
    )(sec, ref, trig, basis, own, full)


def final_kernel(sec_ref, lines_ref, trig_ref, inverse_ref, project_ref, out_ref, sec_mid, ref_mid, sec_time):
    def sec_rows(step, _):
        at = pl.ds(pl.multiple_of(step * 192, 192), 192)
        block = split_value(sec_ref[pl.ds(step * 8, 8)].reshape(192, KEEP))
        result = dot3(block, (inverse_ref[0], inverse_ref[1]))
        for a in range(3):
            sec_mid[a, at, :] = result[:, a * 128 : (a + 1) * 128]
        return 0

    lax.fori_loop(0, 4, sec_rows, 0)

    def pair(tile, group):
        return pltpu.roll(tile, 4, 0) if group else None

    def forward_chunk(a, _):
        for group in range(2):

            def load(n1):
                if group == 0:
                    return lines_ref[n1 * 3 + a, 0:8, :], lines_ref[n1 * 3 + a, 8:16, :]
                tile = lines_ref[n1 * 3 + a, 16:24, :]
                return tile, pair(tile, 1)

            for k1, (re, im) in enumerate(dft32(load, -1)):
                c, s = twiddle(trig_ref, a, k1)
                re, im = re * c + im * s, im * c - re * s
                base = k1 * ROWS
                if group == 0:
                    ref_mid[a, base : base + 8, :] = re
                    ref_mid[a, base + 8 : base + 16, :] = im
                else:
                    ref_mid[a, base + 16 : base + 24, :] = jnp.concatenate([re[0:4], im[0:4]], 0)
        return 0

    lax.fori_loop(0, 3, forward_chunk, 0)

    def ref_rows(step, _):
        at = pl.ds(pl.multiple_of(step * 192, 192), 192)
        block = jnp.concatenate([ref_mid[a, at, :] for a in range(3)], 1)
        result = dot3(split_value(block), (project_ref[0], project_ref[1]))
        for a in range(3):
            ref_mid[a, at, :] = result[:, a * 128 : (a + 1) * 128]
        return 0

    lax.fori_loop(0, 4, ref_rows, 0)

    def untwist(mid, a, group):
        def load(k1):
            base = k1 * ROWS
            c, s = twiddle(trig_ref, a, k1)
            if group == 0:
                re, im = mid[a, base : base + 8, :], mid[a, base + 8 : base + 16, :]
            else:
                re = mid[a, base + 16 : base + 24, :]
                im = pair(re, 1)
            return re * c - im * s, im * c + re * s

        return load

    def last_chunk(a, _):
        for group in range(2):
            count = 8 if group == 0 else 4
            for n1, (re, im) in enumerate(dft32(untwist(sec_mid, a, group), 1)):
                sec_time[0, n1] = re
                sec_time[1, n1] = im
            for n1, (re, im) in enumerate(dft32(untwist(ref_mid, a, group), 1)):
                sr = sec_time[0, n1] * (1.0 / 1024)
                si = sec_time[1, n1] * (1.0 / 1024)
                at = group * 8 * 192 + (n1 * 3 + a) * 2
                out_ref[pl.ds(at, count, stride=192), :] = (sr * re + si * im)[0:count]
                out_ref[pl.ds(at + 1, count, stride=192), :] = (si * re - sr * im)[0:count]
        return 0

    lax.fori_loop(0, 3, last_chunk, 0)


def final(sec_blocks, lines, trig, inverse, project):
    return pl.pallas_call(
        final_kernel,
        out_shape=jax.ShapeDtypeStruct((2 * LINES * 96, 128), F32),
        scratch_shapes=[
            pltpu.VMEM((3, PEERS * ROWS, 128), F32),
            pltpu.VMEM((3, PEERS * ROWS, 128), F32),
            pltpu.VMEM((2, OUTER, 8, 128), F32),
        ],
        compiler_params=pltpu.CompilerParams(vmem_limit_bytes=VMEM_LIMIT),
        name="range_final",
    )(sec_blocks, lines, trig, inverse, project)


def body(reference_slc, secondary_slc, range_start, azimuth_start):
    own, full = azimuth_tables()
    basis, inverse, project = range_tables()
    trig = trig_values(range_start[0], azimuth_start[0], lax.axis_index("line"))
    sec = secondary_slc.reshape(2, LINES, 96, 128).transpose(1, 2, 0, 3).reshape(2 * LINES * 96, 128)
    ref = reference_slc.reshape(2, LINES, 6, 128).transpose(1, 2, 0, 3).reshape(2 * LINES * 6, 128)
    returned, lines = exchange(sec, ref, trig, jnp.asarray(basis), jnp.asarray(own), jnp.asarray(full))
    lines = lines.reshape(96, ROWS, 128)
    out = final(returned, lines, trig, jnp.asarray(inverse), jnp.asarray(project))
    return out.reshape(LINES, 96, 2, 128).transpose(2, 0, 1, 3).reshape(1, 2, LINES, RG)


def solution(mesh):
    in_specs = (P(None, "line", "date"), P("date", None, "line", None), P("date"), P("date"))
    out_specs = P("date", None, "line", None)
    return jax.shard_map(body, mesh=mesh, in_specs=in_specs, out_specs=out_specs, check_vma=False)
```

time: 451 us -> 102 us (0.23); the launches traced: 443 us -> 102 us
  local copies, waits for them, and re-layouts: 181 us -> 1.62 us
  waiting for transfers between devices: 175 us -> 0 us
  Pallas kernels: 0 us -> 96.6 us
  other arithmetic: 35.4 us -> 2.28 us
  matrix products: 21.8 us -> 0 us
  starting transfers between devices: 14.6 us -> 0 us
  between operations: 15.5 us -> 1.31 us
    unnamed x32 -> x0, local copies, waits for them, and re-layouts: 99.9 us -> none
    pallas_call x0 -> x2, Pallas kernels: none -> 96.6 us  [the longest x1 88.1 us: exchange(): pl.pallas_call(exchange_kernel, out_shape=(jax.ShapeDtypeStruct(blocks, F...]
    all_to_all x2 -> x0, waiting for transfers between devices: 93.3 us -> none  [the longest x1 52.5 us: body(): lax.all_to_all(filtered, 'line', split_axis=3, concat_axis=4, tiled=True)]
    all_gather x1 -> x0, waiting for transfers between devices: 81.5 us -> none  [body(): gathered = lax.all_gather(reference_slc, 'date', axis=2, tiled=True)]
    concatenate x1 -> x0, local copies, waits for them, and re-layouts: 23.6 us -> none  [body(): stacked = jnp.concatenate([ref_spec[None], sec_masked], axis=0)]
    all_to_all x4 -> x0, local copies, waits for them, and re-layouts: 23.3 us -> none  [the longest x2 20.6 us: body(): lax.all_to_all(stacked, 'line', split_axis=3, concat_axis=2, tiled=True)]
    dot_general x8 -> x0, matrix products: 21.8 us -> none  [the longest x1 5.98 us: doppler_band(): jnp.einsum('akbn,dsbne->dsake', fwd_block, signals, precision=HIGHEST_PRE...]
    all_to_all x2 -> x0, starting transfers between devices: 14.6 us -> none  [the longest x1 8.19 us: body(): lax.all_to_all(stacked, 'line', split_axis=3, concat_axis=2, tiled=True)]
  transfers between devices with their start and end apart: 3 -> 0, of which waited for: 3 -> 0; matrix products, arithmetic and copies ran while one was open for 5% -> 0% of each run, Pallas kernels for 0% -> 0%
where the time goes in v2:
time: 102 us
  Pallas kernels  96.6 us (95%)
  other arithmetic  2.28 us (2%)
  local copies, waits for them, and re-layouts  1.62 us (2%)
  between operations  1.31 us (1%)
    pallas_call x1, Pallas kernels, exchange(): pl.pallas_call(exchange_kernel, out_shape=(jax.ShapeDtypeStruct(blocks, F...  88.1 us
    pallas_call x1, Pallas kernels, final(): pl.pallas_call(final_kernel, out_shape=jax.ShapeDtypeStruct((2 * LINES *...  8.43 us
    cos x1, other arithmetic, trig_values(): return jnp.cos(turns.astype(F32) * (2 * math.pi / RG))  2.28 us

profile of v2, /device:TPU:1, one launch (start us, length us, event | category | flops | bytes accessed | tf_op | source)
XLA Modules:
  0.0 101.8 jit_solution(16845966292590538771)
XLA Ops:
  1.3 0.9 reshape.29
  2.2 0.7 copy.17
  2.9 2.3 %fusion.8.trig_ref = f32[240,128]{1,0:T(8,128)} fusion(s32[240,128]{1,0:T(8,128)} %constant.66.clone, pred[240,128]{1,0:T(8,128)(4,1)} %constant.77, s32[240,128]{1,0:T(8,128)} %constant.64.clone, pred[240,128]{1,0:T(8,128)(4,1)} %constant.76, s32[240,128]{1,0:T(8,128)} %constant.65.clone, s32[]{:T(128)S(6)} %mul.12, s32[]{:T(128)} %bitcast.6, s32[]{:T(128)} %bitcast.17), kind=kLoop, calls=%fused_computation.14 | loop fusion | flops 829440 | bytes 552972 | tf_op jit(solution)/shard_map/cos | solution.py:158
  5.2 88.1 %exchange.1 = (f32[32,24,256]{2,1,0:T(8,128)}, f32[4,3,8,24,128]{4,3,2,1,0:T(8,128)}) custom-call(f32[2304,128]{1,0:T(8,128)} %bitcast.18, f32[144,128]{1,0:T(8,128)} %bitcast.21, f32[240,128]{1,0:T(8,128)} %fusion.8.trig_ref, bf16[2,384,256]{2,1,0:T(8,128)(2,1)} %constant.67.clone.basis_ref, bf16[2,768,768]{2,1,0:T(8,128)(2,1)} %constant.68.clone.own_hbm, ...), custom_call_target="tpu_custom_call" | custom-call | tf_op jit(solution)/shard_map/exchange/pallas_call | solution.py:461
  93.3 8.4 %range_final.1 = f32[2304,128]{1,0:T(8,128)} custom-call(f32[32,24,256]{2,1,0:T(8,128)} %get-tuple-element.7.sec_ref, f32[96,24,128]{2,1,0:T(8,128)} %bitcast.19, f32[240,128]{1,0:T(8,128)} %fusion.8.trig_ref, bf16[2,256,384]{2,1,0:T(8,128)(2,1)} %constant.70.clone.inverse_ref, bf16[2,384,384]{2,1,0:T(8,128)(2,1)} %constant.71.clone.project_ref), custom_call_target="tpu_custom_call" | custom-call | tf_op jit(solution)/shard_map/range_final/pallas_call | solution.py:565

commit v3 on v2

v3 whole, which is shorter than its diff:
```python
import math

import jax
import jax.numpy as jnp
import ml_dtypes
import numpy as np
from jax import lax
from jax.experimental import pallas as pl
from jax.experimental.pallas import tpu as pltpu
from jax.sharding import PartitionSpec as P

RG = 12288
AZ = 384
OUTER = 32
INNER = 384
KEEP = 256
LINES = 12
ROWS = 24
PEERS = 32
MESH = pl.DeviceIdType.MESH
F32 = jnp.float32
BF16 = jnp.bfloat16
VMEM_LIMIT = 56 * 1024 * 1024


def row_line():
    return np.array(list(range(8)) + list(range(8)) + list(range(8, 12)) * 2)


def row_part():
    return np.array([0] * 8 + [1] * 8 + [0] * 4 + [1] * 4)


def dirichlet(offset, width, length):
    offset = np.asarray(offset)
    safe = np.where(offset == 0, 1, offset)
    value = np.sin(np.pi * width * safe / length) / (length * np.sin(np.pi * safe / length))
    return np.where(offset == 0, width / length, value)


def split_table(table):
    table = np.asarray(table, np.float32)
    high = table.astype(ml_dtypes.bfloat16)
    low = (table - high.astype(np.float32)).astype(ml_dtypes.bfloat16)
    return np.stack([high, low])


def azimuth_tables():
    lines = (np.arange(PEERS)[:, None] * LINES + row_line()[None]).reshape(-1)
    part = np.tile(row_part(), PEERS)
    full = dirichlet(lines[:, None] - lines[None, :], AZ // 2, AZ)
    own = full * (part[:, None] == part[None, :])
    return split_table(own), full.astype(np.float32).reshape(4, 192, 768)


def range_tables():
    n2 = np.arange(INNER)
    angle = 2 * np.pi * (np.arange(KEEP // 2)[None, :] + 0.5) * n2[:, None] / INNER
    basis = math.sqrt(2 / INNER) * np.concatenate([np.cos(angle), np.sin(angle)], 1)
    projection = dirichlet(n2[:, None] - n2[None, :], KEEP, INNER)
    return split_table(basis), split_table(basis.T / OUTER**2), split_table(projection)


def cmul_const(re, im, angle):
    c, s = math.cos(angle), math.sin(angle)
    if abs(c - 1) < 1e-12:
        return re, im
    if abs(c) < 1e-12:
        return (-im, re) if s > 0 else (im, -re)
    if abs(abs(c) - abs(s)) < 1e-12:
        r = math.sqrt(0.5)
        if c > 0 and s > 0:
            return (re - im) * r, (re + im) * r
        if c > 0:
            return (re + im) * r, (im - re) * r
        if s > 0:
            return (re + im) * -r, (re - im) * r
        return (im - re) * r, (re + im) * -r
    return re * c - im * s, re * s + im * c


def dft_small(values, sign):
    n = len(values)
    if n == 1:
        return values
    even = dft_small(values[0::2], sign)
    odd = dft_small(values[1::2], sign)
    low, high = [], []
    for k in range(n // 2):
        tr, ti = cmul_const(odd[k][0], odd[k][1], sign * 2 * math.pi * k / n)
        low.append((even[k][0] + tr, even[k][1] + ti))
        high.append((even[k][0] - tr, even[k][1] - ti))
    return low + high


def dft32(load, sign):
    middle = []
    for q in range(8):
        part = dft_small([load(q + 8 * p) for p in range(4)], sign)
        middle.append([cmul_const(*part[s], sign * 2 * math.pi * q * s / 32) for s in range(4)])
    out = [None] * 32
    for s in range(4):
        part = dft_small([middle[q][s] for q in range(8)], sign)
        for t in range(8):
            out[s + 4 * t] = part[t]
    return out


def split_value(x):
    high = x.astype(BF16)
    low = (x - high.astype(F32)).astype(BF16)
    return high, low


def dot(a, b):
    return jnp.dot(a, b, preferred_element_type=F32)


def dot3(a, b):
    return dot(a[0], b[0]) + dot(a[1], b[0]) + dot(a[0], b[1])


TWIST, VECTOR, PHASE, TRIG = 0, 192, 208, 240


def vector_table():
    table = np.zeros((2, 16, 128), np.float32)
    lines = (np.arange(PEERS)[:, None] * LINES + row_line()[None]).reshape(6, 128)
    real = np.tile(row_part() == 0, PEERS).reshape(6, 128)
    table[0, 0:6] = lines
    table[0, 8:14] = lines
    table[1, 0:6] = np.where(real, 0, -RG // 4)
    table[1, 8:14] = np.where(real, RG // 4, 0)
    return table


def cosine(turns):
    rest = turns - jnp.floor(turns * (1.0 / RG)) * RG
    half = (rest * (1.0 / RG) - 0.5) * math.pi
    square = half * half
    value = jnp.full_like(square, -1.0 / math.factorial(14))
    for k in range(6, -1, -1):
        value = value * square + (-1) ** k / math.factorial(2 * k)
    return 1 - 2 * value * value


def fill_trig(trig_ref, vector_ref, range_first, azimuth_first, line):
    k1 = lax.broadcasted_iota(jnp.int32, (OUTER, 128), 0)
    lane = lax.broadcasted_iota(jnp.int32, (OUTER, 128), 1)
    bins = (range_first + ((k1 - range_first) & (OUTER - 1)) + OUTER * (KEEP - 1) // 2).astype(F32)
    for a in range(3):
        turns = bins * (lane + a * 128).astype(F32)
        trig_ref[a * OUTER : (a + 1) * OUTER, :] = cosine(turns)
        trig_ref[96 + a * OUTER : 96 + (a + 1) * OUTER, :] = cosine(turns - RG // 4)
    factor = ((RG // (2 * AZ)) * (2 * azimuth_first + AZ // 2 - 1)).astype(F32)
    trig_ref[VECTOR : VECTOR + 16, :] = cosine(vector_ref[0] * factor + vector_ref[1])
    turns = (line * LINES + k1[0:16]).astype(F32) * factor
    trig_ref[PHASE : PHASE + 16, :] = cosine(turns)
    trig_ref[PHASE + 16 : PHASE + 32, :] = cosine(turns - RG // 4)


def remote(src, dst, send, recv, date, line):
    return pltpu.make_async_remote_copy(
        src_ref=src, dst_ref=dst, send_sem=send, recv_sem=recv, device_id=(date, line), device_id_type=MESH
    )


def chunk_of(zh, y):
    skip = 3 - y
    return jnp.where(zh > skip, zh - 1, zh), zh != skip


def get_pair(ref, base, group):
    if group == 0:
        return ref[base : base + 8, :], ref[base + 8 : base + 16, :]
    tile = ref[base + 16 : base + 24, :]
    return tile, pltpu.roll(tile, 4, 0)


def put_pair(ref, base, group, re, im):
    if group == 0:
        ref[base : base + 8, :] = re
        ref[base + 8 : base + 16, :] = im
    else:
        ref[base + 16 : base + 24, :] = jnp.concatenate([re[0:4], im[0:4]], 0)


def untwist(mid, trig_ref, a, group):
    def load(k1):
        c, s = twiddle(trig_ref, a, k1)
        re, im = get_pair(mid.at[a], k1 * ROWS, group)
        return re * c - im * s, im * c + re * s

    return load


def twiddle(trig_ref, a, k1):
    row = a * OUTER + k1
    return trig_ref[pl.ds(row, 1), :], trig_ref[pl.ds(96 + row, 1), :]


STEPS = 8
SECOND_AT = 5


def exchange_kernel(
    sec_ref, refr_ref, range_ref, azimuth_ref, vector_ref, basis_ref, inverse_ref, own_hbm, full_hbm,
    time_ref, lines_ref, trig_out,
    trig_ref, mid_ref, coef_ref, spread_ref, chunks_ref, all_ref, vecs_ref, filt_ref, back_ref, rout_ref,
    own_ref, full_ref, mixed_ref,
    a_send, a_recv, b_send, b_recv, x_send, x_recv, v_send, v_recv, y_send, y_recv,
    r_send, r_recv, l_send, l_recv, own_sem, xo_sem,
):
    d, l = lax.axis_index("date"), lax.axis_index("line")
    x, zh = d // 4, d % 4
    zl, u = l // 8, l % 8
    y = u // 2
    z = zh * 4 + zl
    up, down = (z + 1) % 16, (z + 15) % 16
    right = (x * 4 + up // 4, (up % 4) * 8 + u)
    left = (x * 4 + down // 4, (down % 4) * 8 + u)
    place = x * 8 + u
    mine, valid = chunk_of(zh, y)

    own_copy = pltpu.make_async_copy(own_hbm, own_ref, own_sem.at[4])
    own_copy.start()
    full_copy = pltpu.make_async_copy(full_hbm.at[zl], full_ref, own_sem.at[5])
    full_copy.start()

    def plane(i):
        other = (place + i) % PEERS
        ox, ou = other // 8, other % 8
        return other, ox, ou, ox * 4 + zh, zl * 8 + ou

    barrier = pltpu.get_barrier_semaphore()

    def greet(i, _):
        pl.semaphore_signal(barrier, inc=1, device_id=(d, (l + i) % PEERS), device_id_type=MESH)
        _, _, _, od, ol = plane(i)
        pl.semaphore_signal(barrier, inc=1, device_id=(od, ol), device_id_type=MESH)
        return 0

    pl.semaphore_signal(barrier, inc=1, device_id=right, device_id_type=MESH)
    pl.semaphore_signal(barrier, inc=1, device_id=left, device_id_type=MESH)
    lax.fori_loop(1, PEERS, greet, 0)

    for i in range(LINES):
        for part in range(2):
            row = i + 8 * part if i < 8 else 8 + i + 4 * part
            for c in range(6):
                chunks_ref[c, row : row + 1, :] = refr_ref[i, part : part + 1, c * 128 : (c + 1) * 128]

    fill_trig(trig_ref, vector_ref, range_ref[0], azimuth_ref[0], l)
    trig_out[...] = trig_ref[...]

    pl.semaphore_wait(barrier, 2 * (PEERS - 1) + 2)

    def y_slot(i, source):
        return all_ref.at[i, zl, pl.ds(pl.multiple_of(source * ROWS, 8), ROWS)]

    def y_copy(c):
        q = 6 * zh + c
        return remote(chunks_ref.at[c], y_slot(q // 8, u), y_send.at[c], y_recv.at[u], d, zl * 8 + q % 8)

    def y_own(c):
        return pltpu.make_async_copy(chunks_ref.at[c], y_slot((6 * zh + c) // 8, u), own_sem.at[0])

    for c in range(6):
        owner = (6 * zh + c) % 8

        @pl.when(owner != u)
        def _():
            y_copy(c).start()

        @pl.when(owner == u)
        def _():
            y_own(c).start()

    def v_copy(i, slot):
        return remote(
            trig_ref.at[pl.ds(VECTOR, 16)], vecs_ref.at[slot], v_send.at[i], v_recv.at[slot],
            (x + i) % 4 * 4 + zh, l,
        )

    for i in range(1, 4):
        v_copy(i, x).start()
    own_vec = pltpu.make_async_copy(trig_ref.at[pl.ds(VECTOR, 16)], vecs_ref.at[x], own_sem.at[1])
    own_vec.start()

    def chunk(a, _):
        for group in range(2):
            rows = 8 if group == 0 else 4
            first = 8 * group
            pc = trig_ref[PHASE + first : PHASE + first + rows, :]
            ps = trig_ref[PHASE + 16 + first : PHASE + 16 + first + rows, :]

            def load(n1):
                at = first * 192 + (n1 * 3 + a) * 2
                return sec_ref[pl.ds(at, rows, stride=192), :], sec_ref[pl.ds(at + 1, rows, stride=192), :]

            for k1, (re, im) in enumerate(dft32(load, -1)):
                c, s = twiddle(trig_ref, a, k1)
                re, im = re * c + im * s, im * c - re * s
                re, im = re * pc + im * ps, im * pc - re * ps
                put_pair(mid_ref.at[a], k1 * ROWS, group, re, im)
        return 0

    def ring_copy(origin, send, recv, step, to):
        i, ok = chunk_of(origin // 4, y)
        ref = all_ref.at[jnp.where(ok, i, 0), origin % 4]
        return ok, remote(ref, ref, send.at[step], recv.at[step], *to)

    def ring_start(s):
        ok, copy = ring_copy((z + 17 - s) % 16, r_send, r_recv, s, right)
        pl.when(ok)(copy.start)
        if s < STEPS:
            ok2, copy2 = ring_copy((z + s - 1) % 16, l_send, l_recv, s, left)
            pl.when(ok2)(copy2.start)

    def ring_sent(s):
        ok, copy = ring_copy((z + 17 - s) % 16, r_send, r_recv, s, right)
        pl.when(ok)(copy.wait_send)
        if s < STEPS:
            ok2, copy2 = ring_copy((z + s - 1) % 16, l_send, l_recv, s, left)
            pl.when(ok2)(copy2.wait_send)

    def ring_arrived(s):
        ok, copy = ring_copy((z + 16 - s) % 16, r_send, r_recv, s, left)
        pl.when(ok)(copy.wait_recv)
        if s < STEPS:
            ok2, copy2 = ring_copy((z + s) % 16, l_send, l_recv, s, right)
            pl.when(ok2)(copy2.wait_recv)

    def a_copy(to):
        return remote(coef_ref.at[to], spread_ref.at[l], a_send.at[to], a_recv.at[l], d, to)

    def send_blocks(copy, step):
        def send(i, _):
            to = step * 8 + (u + i) % 8
            pl.when(to != l)(copy(to).start)
            return 0

        lax.fori_loop(0, 8, send, 0)

    def rows(k, _):
        step = (zl + 1 + k) % 4
        at = pl.ds(pl.multiple_of(step * 192, 192), 192)
        block = jnp.concatenate([mid_ref[a, at, :] for a in range(3)], 1)
        result = dot3(split_value(block), (basis_ref[0], basis_ref[1]))
        coef_ref[pl.ds(step * 8, 8)] = result.reshape(8, ROWS, KEEP)
        send_blocks(a_copy, step)
        return 0

    def a_own():
        return pltpu.make_async_copy(coef_ref.at[l], spread_ref.at[l], own_sem.at[2])

    def mix():
        row = lax.broadcasted_iota(jnp.int32, (ROWS, 128), 0)
        real = (row < 8) | ((row >= 16) & (row < 20))
        for i in range(1, 4):
            v_copy(i, (x + i) % 4).wait_recv()
        own_vec.wait()
        full_copy.wait()

        def date(t, _):
            at = pl.ds(pl.multiple_of(t * 8 * ROWS, 8 * ROWS), 8 * ROWS)
            for j in range(6):
                lanes = slice(j * 128, (j + 1) * 128)
                mixed = jnp.where(real, vecs_ref[t, j : j + 1, :], vecs_ref[t, 8 + j : 9 + j, :])
                part = (full_ref[:, lanes].reshape(8, ROWS, 128) * mixed[None]).reshape(8 * ROWS, 128)
                high, low = split_value(part)
                mixed_ref[0, at, lanes] = high
                mixed_ref[1, at, lanes] = low
            return 0

        lax.fori_loop(0, 4, date, 0)

    def x_copy(t, i, ou):
        return remote(
            rout_ref.at[t, i, ou], lines_ref.at[x, i, u], x_send.at[(t * 3 + i) * 8 + ou],
            x_recv.at[i * PEERS + place], t * 4 + zh, zl * 8 + ou,
        )

    def x_own(i):
        return pltpu.make_async_copy(rout_ref.at[x, i, u], lines_ref.at[x, i, u], xo_sem.at[i])

    def ref_chunk(block):
        i, ok = chunk_of(block % 4, y)

        @pl.when(ok)
        def _():
            samples = split_value(all_ref[i].reshape(2 * AZ, 128))

            def date(k, _):
                t = (x + 1 + k) % 4
                at = pl.ds(pl.multiple_of(t * 8 * ROWS, 8 * ROWS), 8 * ROWS)
                result = dot3((mixed_ref[0, at, :], mixed_ref[1, at, :]), samples)
                rout_ref[t, i] = result.reshape(8, ROWS, 128)

                def send(j, _):
                    ou = (u + j) % 8
                    pl.when((t != x) | (ou != u))(x_copy(t, i, ou).start)
                    return 0

                lax.fori_loop(0, 8, send, 0)
                return 0

            lax.fori_loop(0, 4, date, 0)
            x_own(i).start()

    def b_copy(to):
        return remote(filt_ref.at[to], back_ref.at[l], b_send.at[to], b_recv.at[l], d, to)

    def b_own():
        return pltpu.make_async_copy(filt_ref.at[l], back_ref.at[l], own_sem.at[3])

    def second():
        a_own().wait()
        own_copy.wait()

        def arrived(i, _):
            source = (l + i) % PEERS
            remote(
                coef_ref.at[source], spread_ref.at[source], a_send.at[source], a_recv.at[source], d, source
            ).wait_recv()
            return 0

        lax.fori_loop(1, PEERS, arrived, 0)
        sec = split_value(spread_ref[...].reshape(PEERS * ROWS, KEEP))

        def sec_rows(k, _):
            step = (zl + 1 + k) % 4
            at = pl.ds(pl.multiple_of(step * 192, 192), 192)
            result = dot3((own_ref[0, at, :], own_ref[1, at, :]), sec)
            filt_ref[pl.ds(step * 8, 8)] = result.reshape(8, ROWS, KEEP)
            send_blocks(b_copy, step)
            return 0

        lax.fori_loop(0, 4, sec_rows, 0)
        b_own().start()

    def inverse():
        b_own().wait()

        def arrived(i, _):
            source = (l + i) % PEERS
            remote(
                filt_ref.at[source], back_ref.at[source], b_send.at[source], b_recv.at[source], d, source
            ).wait_recv()
            return 0

        lax.fori_loop(1, PEERS, arrived, 0)

        def inverse_rows(step, _):
            at = pl.ds(pl.multiple_of(step * 192, 192), 192)
            block = split_value(back_ref[pl.ds(step * 8, 8)].reshape(192, KEEP))
            result = dot3(block, (inverse_ref[0], inverse_ref[1]))
            for a in range(3):
                mid_ref[a, at, :] = result[:, a * 128 : (a + 1) * 128]
            return 0

        lax.fori_loop(0, 4, inverse_rows, 0)

        def time_chunk(a, _):
            for group in range(2):
                for n1, (re, im) in enumerate(dft32(untwist(mid_ref, trig_ref, a, group), 1)):
                    put_pair(time_ref.at[n1 * 3 + a], 0, group, re, im)
            return 0

        lax.fori_loop(0, 3, time_chunk, 0)

    chunk(0, 0)

    @pl.when(valid)
    def _():
        for i in range(1, 8):
            source = (u + i) % 8
            remote(
                chunks_ref.at[0], y_slot(mine, source), y_send.at[0], y_recv.at[source], d, zl * 8 + source
            ).wait_recv()
        y_own(0).wait()

    ring_start(1)
    lax.fori_loop(1, 3, chunk, 0)
    ring_arrived(1)
    ring_start(2)
    lax.fori_loop(0, 4, rows, 0)
    a_own().start()
    mix()
    for s in range(2, STEPS + 1):
        ring_arrived(s)
        if s < STEPS:
            ring_start(s + 1)
        if s == 3:
            ref_chunk(zh)
        if s == SECOND_AT:
            second()
        if s == STEPS - 1:
            ref_chunk(zh + 1)
            ref_chunk(zh + 3)
    ref_chunk(zh + 2)
    inverse()

    for s in range(1, STEPS + 1):
        ring_sent(s)
    for i in range(1, 4):
        v_copy(i, x).wait_send()
    for c in range(6):
        owner = (6 * zh + c) % 8

        @pl.when(owner != u)
        def _():
            y_copy(c).wait_send()

    def finish(k, _):
        other, ox, ou, od, ol = plane(k)
        for i in range(3):
            copy = remote(
                rout_ref.at[ox, i, ou], lines_ref.at[ox, i, ou], x_send.at[(ox * 3 + i) * 8 + ou],
                x_recv.at[i * PEERS + other], od, ol,
            )
            copy.wait_send()
            copy.wait_recv()
        to = (l + k) % PEERS
        a_copy(to).wait_send()
        b_copy(to).wait_send()
        return 0

    for i in range(3):
        x_own(i).wait()
    lax.fori_loop(1, PEERS, finish, 0)


def exchange(sec, ref, range_start, azimuth_start, vector, basis, inverse, own, full):
    any_space = pl.BlockSpec(memory_space=pl.ANY)
    vmem = pl.BlockSpec(memory_space=pltpu.VMEM)
    smem = pl.BlockSpec(memory_space=pltpu.SMEM)
    dma = pltpu.SemaphoreType.DMA
    blocks = (PEERS, ROWS, KEEP)
    lines = (4, 3, 8, ROWS, 128)
    peers = dma((PEERS,))
    ring = dma((STEPS + 1,))
    return pl.pallas_call(
        exchange_kernel,
        out_shape=(
            jax.ShapeDtypeStruct((96, ROWS, 128), F32),
            jax.ShapeDtypeStruct(lines, F32),
            jax.ShapeDtypeStruct((TRIG, 128), F32),
        ),
        in_specs=[vmem, vmem, smem, smem, vmem, vmem, vmem, any_space, any_space],
        out_specs=(vmem, any_space, vmem),
        scratch_shapes=[
            pltpu.VMEM((TRIG, 128), F32),
            pltpu.VMEM((3, PEERS * ROWS, 128), F32),
            pltpu.VMEM(blocks, F32),
            pltpu.VMEM(blocks, F32),
            pltpu.VMEM((6, ROWS, 128), F32),
            pltpu.VMEM((3, 4, 8 * ROWS, 128), F32),
            pltpu.VMEM((4, 16, 128), F32),
            pltpu.VMEM(blocks, F32),
            pltpu.VMEM(blocks, F32),
            pltpu.VMEM(lines, F32),
            pltpu.VMEM((2, 2 * AZ, 2 * AZ), BF16),
            pltpu.VMEM((8 * ROWS, 2 * AZ), F32),
            pltpu.VMEM((2, 2 * AZ, 2 * AZ), BF16),
            peers, peers, peers, peers, dma((3 * PEERS,)), dma((3 * PEERS,)),
            dma((4,)), dma((4,)), dma((6,)), dma((8,)),
            ring, ring, ring, ring, dma((6,)), dma((3,)),
        ],
        compiler_params=pltpu.CompilerParams(
            collective_id=1, has_side_effects=True, vmem_limit_bytes=VMEM_LIMIT
        ),
        name="exchange",
    )(sec, ref, range_start, azimuth_start, vector, basis, inverse, own, full)


def final_kernel(time_ref, lines_ref, trig_ref, project_ref, out_ref, mid_ref):
    def forward_chunk(a, _):
        for group in range(2):

            def load(n1):
                return get_pair(lines_ref.at[n1 * 3 + a], 0, group)

            for k1, (re, im) in enumerate(dft32(load, -1)):
                c, s = twiddle(trig_ref, a, k1)
                put_pair(mid_ref.at[a], k1 * ROWS, group, re * c + im * s, im * c - re * s)
        return 0

    lax.fori_loop(0, 3, forward_chunk, 0)

    def rows(step, _):
        at = pl.ds(pl.multiple_of(step * 192, 192), 192)
        block = jnp.concatenate([mid_ref[a, at, :] for a in range(3)], 1)
        result = dot3(split_value(block), (project_ref[0], project_ref[1]))
        for a in range(3):
            mid_ref[a, at, :] = result[:, a * 128 : (a + 1) * 128]
        return 0

    lax.fori_loop(0, 4, rows, 0)

    def last_chunk(a, _):
        for group in range(2):
            count = 8 if group == 0 else 4
            for n1, (re, im) in enumerate(dft32(untwist(mid_ref, trig_ref, a, group), 1)):
                sr, si = get_pair(time_ref.at[n1 * 3 + a], 0, group)
                at = group * 8 * 192 + (n1 * 3 + a) * 2
                out_ref[pl.ds(at, count, stride=192), :] = (sr * re + si * im)[0:count]
                out_ref[pl.ds(at + 1, count, stride=192), :] = (si * re - sr * im)[0:count]
        return 0

    lax.fori_loop(0, 3, last_chunk, 0)


def final(time, lines, trig, project):
    return pl.pallas_call(
        final_kernel,
        out_shape=jax.ShapeDtypeStruct((2 * LINES * 96, 128), F32),
        scratch_shapes=[pltpu.VMEM((3, PEERS * ROWS, 128), F32)],
        compiler_params=pltpu.CompilerParams(vmem_limit_bytes=VMEM_LIMIT),
        name="range_final",
    )(time, lines, trig, project)


def body(reference_slc, secondary_slc, range_start, azimuth_start):
    own, full = (jnp.asarray(t) for t in azimuth_tables())
    basis, inverse, project = (jnp.asarray(t) for t in range_tables())
    sec = secondary_slc.reshape(2, LINES, 96, 128).transpose(1, 2, 0, 3).reshape(2 * LINES * 96, 128)
    ref = reference_slc.transpose(1, 0, 2)
    time, lines, trig = exchange(
        sec, ref, range_start, azimuth_start, jnp.asarray(vector_table()), basis, inverse, own, full
    )
    out = final(time, lines.reshape(96, ROWS, 128), trig, project)
    return out.reshape(LINES, 96, 2, 128).transpose(2, 0, 1, 3).reshape(1, 2, LINES, RG)


def solution(mesh):
    in_specs = (P(None, "line", "date"), P("date", None, "line", None), P("date"), P("date"))
    out_specs = P("date", None, "line", None)
    return jax.shard_map(body, mesh=mesh, in_specs=in_specs, out_specs=out_specs, check_vma=False)
```

time: 102 us -> 99.8 us (0.978)
  the two profiles are of different devices: /device:TPU:1 before, /device:TPU:41 now
where the time goes in v3:
time: 99.8 us; the launch traced here: 99.6 us
  Pallas kernels  98.3 us (98%)
  between operations  1.3 us (1%)
    pallas_call x1, Pallas kernels, exchange(): pl.pallas_call(exchange_kernel, out_shape=(jax.ShapeDtypeStruct((96, ROWS...  91.8 us
    pallas_call x1, Pallas kernels, final(): pl.pallas_call(final_kernel, out_shape=jax.ShapeDtypeStruct((2 * LINES *...  6.46 us

profile of v3, /device:TPU:41, one launch (start us, length us, event | category | flops | bytes accessed | tf_op | source)
XLA Modules:
  0.0 99.6 jit_solution(16320437594543632188)
XLA Ops:
  1.3 91.8 %exchange.1 = (f32[96,24,128]{2,1,0:T(8,128)}, f32[4,3,8,24,128]{4,3,2,1,0:T(8,128)}, f32[240,128]{1,0:T(8,128)}) custom-call(f32[2304,128]{1,0:T(8,128)} %bitcast.12, f32[12,2,768]{2,1,0:T(2,128)} %bitcast.14, s32[1]{0:T(128)S(6)} %copy.13.range_ref, s32[1]{0:T(128)S(6)} %copy.14.azimuth_ref, f32[2,16,128]{2,1,0:T(8,128)} %constant.17.clone.vector_ref, ...), custom_call_target="tpu_custom_call" | custom-call | tf_op jit(solution)/shard_map/exchange/pallas_call | solution.py:543
  93.1 6.5 %range_final.1 = f32[2304,128]{1,0:T(8,128)} custom-call(f32[96,24,128]{2,1,0:T(8,128)} %get-tuple-element.8.time_ref, f32[96,24,128]{2,1,0:T(8,128)} %bitcast.13, f32[240,128]{1,0:T(8,128)} %get-tuple-element.10.trig_ref, bf16[2,384,384]{2,1,0:T(8,128)(2,1)} %constant.16.clone.project_ref), custom_call_target="tpu_custom_call" | custom-call | tf_op jit(solution)/shard_map/range_final/pallas_call | solution.py:615

commit v4 on v3

--- a/solution.py
+++ b/solution.py
@@ -200,13 +200,14 @@
 
 
 STEPS = 8
-SECOND_AT = 5
+PIECES = 2
+PIECE = 8 * ROWS // PIECES
 
 
 def exchange_kernel(
-    sec_ref, refr_ref, range_ref, azimuth_ref, vector_ref, basis_ref, inverse_ref, own_hbm, full_hbm,
-    time_ref, lines_ref, trig_out,
-    trig_ref, mid_ref, coef_ref, spread_ref, chunks_ref, all_ref, vecs_ref, filt_ref, back_ref, rout_ref,
+    sec_ref, refr_ref, range_ref, azimuth_ref, vector_ref, basis_ref, project_ref, own_hbm, full_hbm,
+    back_ref, time_out, trig_out,
+    trig_ref, mid_ref, coef_ref, spread_ref, chunks_ref, all_ref, vecs_ref, filt_ref, lines_ref, time_ref, rout_ref,
     own_ref, full_ref, mixed_ref,
     a_send, a_recv, b_send, b_recv, x_send, x_recv, v_send, v_recv, y_send, y_recv,
     r_send, r_recv, l_send, l_recv, own_sem, xo_sem,
@@ -305,31 +306,39 @@
                 put_pair(mid_ref.at[a], k1 * ROWS, group, re, im)
         return 0
 
-    def ring_copy(origin, send, recv, step, to):
+    def ring_copy(origin, send, recv, step, piece, to):
         i, ok = chunk_of(origin // 4, y)
-        ref = all_ref.at[jnp.where(ok, i, 0), origin % 4]
-        return ok, remote(ref, ref, send.at[step], recv.at[step], *to)
-
-    def ring_start(s):
-        ok, copy = ring_copy((z + 17 - s) % 16, r_send, r_recv, s, right)
+        ref = all_ref.at[jnp.where(ok, i, 0), origin % 4, pl.ds(piece * PIECE, PIECE)]
+        at = step * PIECES + piece
+        return ok, remote(ref, ref, send.at[at], recv.at[at], *to)
+
+    def ring_start(s, p):
+        ok, copy = ring_copy((z + 17 - s) % 16, r_send, r_recv, s, p, right)
         pl.when(ok)(copy.start)
         if s < STEPS:
-            ok2, copy2 = ring_copy((z + s - 1) % 16, l_send, l_recv, s, left)
+            ok2, copy2 = ring_copy((z + s - 1) % 16, l_send, l_recv, s, p, left)
             pl.when(ok2)(copy2.start)
 
-    def ring_sent(s):
-        ok, copy = ring_copy((z + 17 - s) % 16, r_send, r_recv, s, right)
+    def ring_sent(s, p):
+        ok, copy = ring_copy((z + 17 - s) % 16, r_send, r_recv, s, p, right)
         pl.when(ok)(copy.wait_send)
         if s < STEPS:
-            ok2, copy2 = ring_copy((z + s - 1) % 16, l_send, l_recv, s, left)
+            ok2, copy2 = ring_copy((z + s - 1) % 16, l_send, l_recv, s, p, left)
             pl.when(ok2)(copy2.wait_send)
 
-    def ring_arrived(s):
-        ok, copy = ring_copy((z + 16 - s) % 16, r_send, r_recv, s, left)
+    def ring_arrived(s, p):
+        ok, copy = ring_copy((z + 16 - s) % 16, r_send, r_recv, s, p, left)
         pl.when(ok)(copy.wait_recv)
         if s < STEPS:
-            ok2, copy2 = ring_copy((z + s) % 16, l_send, l_recv, s, right)
+            ok2, copy2 = ring_copy((z + s) % 16, l_send, l_recv, s, p, right)
             pl.when(ok2)(copy2.wait_recv)
+
+    def ring_step(s):
+        for p in range(PIECES):
+            if s > 1:
+                ring_arrived(s - 1, p)
+            if s <= STEPS:
+                ring_start(s, p)
 
     def a_copy(to):
         return remote(coef_ref.at[to], spread_ref.at[l], a_send.at[to], a_recv.at[l], d, to)
@@ -343,13 +352,24 @@
         lax.fori_loop(0, 8, send, 0)
 
     def rows(k, _):
-        step = (zl + 1 + k) % 4
+        step = (zl + k) % 4
         at = pl.ds(pl.multiple_of(step * 192, 192), 192)
         block = jnp.concatenate([mid_ref[a, at, :] for a in range(3)], 1)
         result = dot3(split_value(block), (basis_ref[0], basis_ref[1]))
         coef_ref[pl.ds(step * 8, 8)] = result.reshape(8, ROWS, KEEP)
-        send_blocks(a_copy, step)
         return 0
+
+    def cross(k, _):
+        send_blocks(a_copy, (zl + k) % 4)
+        return 0
+
+    def cross_part(part):
+        def send(n, _):
+            copy = a_copy((zl + 1 + n // 8) % 4 * 8 + (u + n) % 8)
+            copy.start()
+            return 0
+
+        lax.fori_loop(4 * part, 4 * part + 4, send, 0)
 
     def a_own():
         return pltpu.make_async_copy(coef_ref.at[l], spread_ref.at[l], own_sem.at[2])
@@ -377,12 +397,12 @@
 
     def x_copy(t, i, ou):
         return remote(
-            rout_ref.at[t, i, ou], lines_ref.at[x, i, u], x_send.at[(t * 3 + i) * 8 + ou],
+            rout_ref.at[t, i, ou], lines_ref.at[x * 24 + i * 8 + u], x_send.at[(t * 3 + i) * 8 + ou],
             x_recv.at[i * PEERS + place], t * 4 + zh, zl * 8 + ou,
         )
 
     def x_own(i):
-        return pltpu.make_async_copy(rout_ref.at[x, i, u], lines_ref.at[x, i, u], xo_sem.at[i])
+        return pltpu.make_async_copy(rout_ref.at[x, i, u], lines_ref.at[x * 24 + i * 8 + u], xo_sem.at[i])
 
     def ref_chunk(block):
         i, ok = chunk_of(block % 4, y)
@@ -439,27 +459,48 @@
         lax.fori_loop(0, 4, sec_rows, 0)
         b_own().start()
 
-    def inverse():
-        b_own().wait()
-
-        def arrived(i, _):
-            source = (l + i) % PEERS
-            remote(
-                filt_ref.at[source], back_ref.at[source], b_send.at[source], b_recv.at[source], d, source
-            ).wait_recv()
-            return 0
-
+    def x_other(k, i):
+        other, ox, ou, od, ol = plane(k)
+        return remote(
+            rout_ref.at[ox, i, ou], lines_ref.at[ox * 24 + i * 8 + ou], x_send.at[(ox * 3 + i) * 8 + ou],
+            x_recv.at[i * PEERS + other], od, ol,
+        )
+
+    def time_copy():
+        return pltpu.make_async_copy(time_ref, time_out, own_sem.at[1])
+
+    def ref_range():
+        def arrived(k, _):
+            for i in range(3):
+                x_other(k, i).wait_recv()
+            return 0
+
+        for i in range(3):
+            x_own(i).wait()
         lax.fori_loop(1, PEERS, arrived, 0)
 
-        def inverse_rows(step, _):
+        def forward_chunk(a, _):
+            for group in range(2):
+
+                def load(n1):
+                    return get_pair(lines_ref.at[n1 * 3 + a], 0, group)
+
+                for k1, (re, im) in enumerate(dft32(load, -1)):
+                    c, s = twiddle(trig_ref, a, k1)
+                    put_pair(mid_ref.at[a], k1 * ROWS, group, re * c + im * s, im * c - re * s)
+            return 0
+
+        lax.fori_loop(0, 3, forward_chunk, 0)
+
+        def project_rows(step, _):
             at = pl.ds(pl.multiple_of(step * 192, 192), 192)
-            block = split_value(back_ref[pl.ds(step * 8, 8)].reshape(192, KEEP))
-            result = dot3(block, (inverse_ref[0], inverse_ref[1]))
+            block = jnp.concatenate([mid_ref[a, at, :] for a in range(3)], 1)
+            result = dot3(split_value(block), (project_ref[0], project_ref[1]))
             for a in range(3):
                 mid_ref[a, at, :] = result[:, a * 128 : (a + 1) * 128]
             return 0
 
-        lax.fori_loop(0, 4, inverse_rows, 0)
+        lax.fori_loop(0, 4, project_rows, 0)
 
         def time_chunk(a, _):
             for group in range(2):
@@ -468,6 +509,7 @@
             return 0
 
         lax.fori_loop(0, 3, time_chunk, 0)
+        time_copy().start()
 
     chunk(0, 0)
 
@@ -480,29 +522,30 @@
             ).wait_recv()
         y_own(0).wait()
 
-    ring_start(1)
+    ring_step(1)
     lax.fori_loop(1, 3, chunk, 0)
-    ring_arrived(1)
-    ring_start(2)
+    ring_step(2)
     lax.fori_loop(0, 4, rows, 0)
     a_own().start()
+    cross(0, 0)
     mix()
-    for s in range(2, STEPS + 1):
-        ring_arrived(s)
-        if s < STEPS:
-            ring_start(s + 1)
-        if s == 3:
+    for s in range(3, STEPS + 1):
+        ring_step(s)
+        if s - 3 < 6:
+            cross_part(s - 3)
+        if s == 4:
             ref_chunk(zh)
-        if s == SECOND_AT:
+        if s == 99:
             second()
-        if s == STEPS - 1:
-            ref_chunk(zh + 1)
-            ref_chunk(zh + 3)
+    ref_chunk(zh + 1)
+    ref_chunk(zh + 3)
+    second()
+    ring_step(STEPS + 1)
     ref_chunk(zh + 2)
-    inverse()
-
+    ref_range()
     for s in range(1, STEPS + 1):
-        ring_sent(s)
+        for p in range(PIECES):
+            ring_sent(s, p)
     for i in range(1, 4):
         v_copy(i, x).wait_send()
     for c in range(6):
@@ -513,42 +556,37 @@
             y_copy(c).wait_send()
 
     def finish(k, _):
-        other, ox, ou, od, ol = plane(k)
         for i in range(3):
-            copy = remote(
-                rout_ref.at[ox, i, ou], lines_ref.at[ox, i, ou], x_send.at[(ox * 3 + i) * 8 + ou],
-                x_recv.at[i * PEERS + other], od, ol,
-            )
-            copy.wait_send()
-            copy.wait_recv()
+            x_other(k, i).wait_send()
         to = (l + k) % PEERS
         a_copy(to).wait_send()
         b_copy(to).wait_send()
+        remote(filt_ref.at[to], back_ref.at[to], b_send.at[to], b_recv.at[to], d, to).wait_recv()
         return 0
 
-    for i in range(3):
-        x_own(i).wait()
     lax.fori_loop(1, PEERS, finish, 0)
-
-
-def exchange(sec, ref, range_start, azimuth_start, vector, basis, inverse, own, full):
+    b_own().wait()
+    time_copy().wait()
+
+
+def exchange(sec, ref, range_start, azimuth_start, vector, basis, project, own, full):
     any_space = pl.BlockSpec(memory_space=pl.ANY)
     vmem = pl.BlockSpec(memory_space=pltpu.VMEM)
     smem = pl.BlockSpec(memory_space=pltpu.SMEM)
     dma = pltpu.SemaphoreType.DMA
     blocks = (PEERS, ROWS, KEEP)
-    lines = (4, 3, 8, ROWS, 128)
+    time = (96, ROWS, 128)
     peers = dma((PEERS,))
-    ring = dma((STEPS + 1,))
+    ring = dma(((STEPS + 1) * PIECES,))
     return pl.pallas_call(
         exchange_kernel,
         out_shape=(
-            jax.ShapeDtypeStruct((96, ROWS, 128), F32),
-            jax.ShapeDtypeStruct(lines, F32),
+            jax.ShapeDtypeStruct(blocks, F32),
+            jax.ShapeDtypeStruct(time, F32),
             jax.ShapeDtypeStruct((TRIG, 128), F32),
         ),
         in_specs=[vmem, vmem, smem, smem, vmem, vmem, vmem, any_space, any_space],
-        out_specs=(vmem, any_space, vmem),
+        out_specs=(any_space, any_space, vmem),
         scratch_shapes=[
             pltpu.VMEM((TRIG, 128), F32),
             pltpu.VMEM((3, PEERS * ROWS, 128), F32),
@@ -558,8 +596,9 @@
             pltpu.VMEM((3, 4, 8 * ROWS, 128), F32),
             pltpu.VMEM((4, 16, 128), F32),
             pltpu.VMEM(blocks, F32),
-            pltpu.VMEM(blocks, F32),
-            pltpu.VMEM(lines, F32),
+            pltpu.VMEM(time, F32),
+            pltpu.VMEM(time, F32),
+            pltpu.VMEM((4, 3, 8, ROWS, 128), F32),
             pltpu.VMEM((2, 2 * AZ, 2 * AZ), BF16),
             pltpu.VMEM((8 * ROWS, 2 * AZ), F32),
             pltpu.VMEM((2, 2 * AZ, 2 * AZ), BF16),
@@ -571,27 +610,14 @@
             collective_id=1, has_side_effects=True, vmem_limit_bytes=VMEM_LIMIT
         ),
         name="exchange",
-    )(sec, ref, range_start, azimuth_start, vector, basis, inverse, own, full)
-
-
-def final_kernel(time_ref, lines_ref, trig_ref, project_ref, out_ref, mid_ref):
-    def forward_chunk(a, _):
-        for group in range(2):
-
-            def load(n1):
-                return get_pair(lines_ref.at[n1 * 3 + a], 0, group)
-
-            for k1, (re, im) in enumerate(dft32(load, -1)):
-                c, s = twiddle(trig_ref, a, k1)
-                put_pair(mid_ref.at[a], k1 * ROWS, group, re * c + im * s, im * c - re * s)
-        return 0
-
-    lax.fori_loop(0, 3, forward_chunk, 0)
-
+    )(sec, ref, range_start, azimuth_start, vector, basis, project, own, full)
+
+
+def final_kernel(back_ref, time_ref, trig_ref, inverse_ref, out_ref, mid_ref):
     def rows(step, _):
         at = pl.ds(pl.multiple_of(step * 192, 192), 192)
-        block = jnp.concatenate([mid_ref[a, at, :] for a in range(3)], 1)
-        result = dot3(split_value(block), (project_ref[0], project_ref[1]))
+        block = split_value(back_ref[pl.ds(step * 8, 8)].reshape(192, KEEP))
+        result = dot3(block, (inverse_ref[0], inverse_ref[1]))
         for a in range(3):
             mid_ref[a, at, :] = result[:, a * 128 : (a + 1) * 128]
         return 0
@@ -601,8 +627,8 @@
     def last_chunk(a, _):
         for group in range(2):
             count = 8 if group == 0 else 4
-            for n1, (re, im) in enumerate(dft32(untwist(mid_ref, trig_ref, a, group), 1)):
-                sr, si = get_pair(time_ref.at[n1 * 3 + a], 0, group)
+            for n1, (sr, si) in enumerate(dft32(untwist(mid_ref, trig_ref, a, group), 1)):
+                re, im = get_pair(time_ref.at[n1 * 3 + a], 0, group)
                 at = group * 8 * 192 + (n1 * 3 + a) * 2
                 out_ref[pl.ds(at, count, stride=192), :] = (sr * re + si * im)[0:count]
                 out_ref[pl.ds(at + 1, count, stride=192), :] = (si * re - sr * im)[0:count]
@@ -611,14 +637,14 @@
     lax.fori_loop(0, 3, last_chunk, 0)
 
 
-def final(time, lines, trig, project):
+def final(back, time, trig, inverse):
     return pl.pallas_call(
         final_kernel,
         out_shape=jax.ShapeDtypeStruct((2 * LINES * 96, 128), F32),
         scratch_shapes=[pltpu.VMEM((3, PEERS * ROWS, 128), F32)],
         compiler_params=pltpu.CompilerParams(vmem_limit_bytes=VMEM_LIMIT),
         name="range_final",
-    )(time, lines, trig, project)
+    )(back, time, trig, inverse)
 
 
 def body(reference_slc, secondary_slc, range_start, azimuth_start):
@@ -626,10 +652,10 @@
     basis, inverse, project = (jnp.asarray(t) for t in range_tables())
     sec = secondary_slc.reshape(2, LINES, 96, 128).transpose(1, 2, 0, 3).reshape(2 * LINES * 96, 128)
     ref = reference_slc.transpose(1, 0, 2)
-    time, lines, trig = exchange(
-        sec, ref, range_start, azimuth_start, jnp.asarray(vector_table()), basis, inverse, own, full
+    back, time, trig = exchange(
+        sec, ref, range_start, azimuth_start, jnp.asarray(vector_table()), basis, project, own, full
     )
-    out = final(time, lines.reshape(96, ROWS, 128), trig, project)
+    out = final(back, time, trig, inverse)
     return out.reshape(LINES, 96, 2, 128).transpose(2, 0, 1, 3).reshape(1, 2, LINES, RG)
 
 

time: 99.8 us -> 92.8 us (0.930)
  the two profiles are of different devices: /device:TPU:41 before, /device:TPU:1 now
where the time goes in v4:
time: 92.8 us; the launch traced here: 92 us
  Pallas kernels  90.7 us (98%)
  between operations  1.3 us (1%)
    pallas_call x1, Pallas kernels, exchange(): pl.pallas_call(exchange_kernel, out_shape=(jax.ShapeDtypeStruct(blocks, F...  85.5 us
    pallas_call x1, Pallas kernels, final(): pl.pallas_call(final_kernel, out_shape=jax.ShapeDtypeStruct((2 * LINES *...  5.19 us

profile of v4, /device:TPU:1, one launch (start us, length us, event | category | flops | bytes accessed | tf_op | source)
XLA Modules:
  0.0 92.0 jit_solution(4448960237978960943)
XLA Ops:
  1.3 85.5 %exchange.1 = (f32[32,24,256]{2,1,0:T(8,128)}, f32[96,24,128]{2,1,0:T(8,128)}, f32[240,128]{1,0:T(8,128)}) custom-call(f32[2304,128]{1,0:T(8,128)} %bitcast.11, f32[12,2,768]{2,1,0:T(2,128)} %bitcast.12, s32[1]{0:T(128)S(6)} %copy.13.range_ref, s32[1]{0:T(128)S(6)} %copy.14.azimuth_ref, f32[2,16,128]{2,1,0:T(8,128)} %constant.17.clone.vector_ref, ...), custom_call_target="tpu_custom_call" | custom-call | tf_op jit(solution)/shard_map/exchange/pallas_call | solution.py:581
  86.8 5.2 %range_final.1 = f32[2304,128]{1,0:T(8,128)} custom-call(f32[32,24,256]{2,1,0:T(8,128)} %get-tuple-element.8.back_ref, f32[96,24,128]{2,1,0:T(8,128)} %get-tuple-element.9.time_ref, f32[240,128]{1,0:T(8,128)} %get-tuple-element.10.trig_ref, bf16[2,256,384]{2,1,0:T(8,128)(2,1)} %constant.15.clone.inverse_ref), custom_call_target="tpu_custom_call" | custom-call | tf_op jit(solution)/shard_map/range_final/pallas_call | solution.py:641

commit v5 on v4

--- a/solution.py
+++ b/solution.py
@@ -369,7 +369,7 @@
             copy.start()
             return 0
 
-        lax.fori_loop(4 * part, 4 * part + 4, send, 0)
+        lax.fori_loop(3 * part, 3 * part + 3 if part < 5 else 24, send, 0)
 
     def a_own():
         return pltpu.make_async_copy(coef_ref.at[l], spread_ref.at[l], own_sem.at[2])
@@ -535,13 +535,12 @@
             cross_part(s - 3)
         if s == 4:
             ref_chunk(zh)
-        if s == 99:
-            second()
-    ref_chunk(zh + 1)
-    ref_chunk(zh + 3)
-    second()
+        if s == 6:
+            ref_chunk(zh + jnp.where(zl >= 2, 1, 3))
+    ref_chunk(zh + jnp.where(zl >= 2, 3, 1))
     ring_step(STEPS + 1)
     ref_chunk(zh + 2)
+    second()
     ref_range()
     for s in range(1, STEPS + 1):
         for p in range(PIECES):

time: 92.8 us -> 91.1 us (0.982)
  Pallas kernels: 90.7 us -> 89.3 us
    pallas_call x1, Pallas kernels: 85.5 us -> 84.1 us  [exchange(): pl.pallas_call(exchange_kernel, out_shape=(jax.ShapeDtypeStruct(blocks, F...]
where the time goes in v5:
time: 91.1 us; the launch traced here: 90.6 us
  Pallas kernels  89.3 us (98%)
  between operations  1.3 us (1%)
    pallas_call x1, Pallas kernels, exchange(): pl.pallas_call(exchange_kernel, out_shape=(jax.ShapeDtypeStruct(blocks, F...  84.1 us
    pallas_call x1, Pallas kernels, final(): pl.pallas_call(final_kernel, out_shape=jax.ShapeDtypeStruct((2 * LINES *...  5.19 us

profile of v5, /device:TPU:1, one launch (start us, length us, event | category | flops | bytes accessed | tf_op | source)
XLA Modules:
  0.0 90.6 jit_solution(11908264552889859562)
XLA Ops:
  1.3 84.1 %exchange.1 = (f32[32,24,256]{2,1,0:T(8,128)}, f32[96,24,128]{2,1,0:T(8,128)}, f32[240,128]{1,0:T(8,128)}) custom-call(f32[2304,128]{1,0:T(8,128)} %bitcast.11, f32[12,2,768]{2,1,0:T(2,128)} %bitcast.12, s32[1]{0:T(128)S(6)} %copy.13.range_ref, s32[1]{0:T(128)S(6)} %copy.14.azimuth_ref, f32[2,16,128]{2,1,0:T(8,128)} %constant.17.clone.vector_ref, ...), custom_call_target="tpu_custom_call" | custom-call | tf_op jit(solution)/shard_map/exchange/pallas_call | solution.py:580
  85.4 5.2 %range_final.1 = f32[2304,128]{1,0:T(8,128)} custom-call(f32[32,24,256]{2,1,0:T(8,128)} %get-tuple-element.8.back_ref, f32[96,24,128]{2,1,0:T(8,128)} %get-tuple-element.9.time_ref, f32[240,128]{1,0:T(8,128)} %get-tuple-element.10.trig_ref, bf16[2,256,384]{2,1,0:T(8,128)(2,1)} %constant.15.clone.inverse_ref), custom_call_target="tpu_custom_call" | custom-call | tf_op jit(solution)/shard_map/range_final/pallas_call | solution.py:640
